TPU v7x, 256 devices: a whole 4x4x8 slice. The times are simulated.
256 devices in a mesh: dp: 16 (over z, core), expert: 4 (over x), tensor: 4 (over y).
Axes of the slice: x: 4, y: 4, z: 8, core: 2. Of those that a mesh axis runs over, the one named last changes fastest.
Arguments:
- tokens: bfloat16 [8192, 2048], P(('dp', 'expert', 'tensor')), may hold values from -6 to 6
- out_grad: bfloat16 [8192, 2048], P(('dp', 'expert', 'tensor')), may hold values from -6 to 6
- routes: int32 [8192, 6], P(('dp', 'expert', 'tensor')), may hold values from 0 to 63, all different within a row; in each aligned block of 32 rows (0 to 31, 32 to 63, ...) at most 4 rows name the same one
- gates: bfloat16 [8192, 6], P(('dp', 'expert', 'tensor')), may hold values from 0.099609375 to 1
- w_gate: bfloat16 [64, 2048, 1408], P(('dp', 'expert'), None, 'tensor'), may hold values from -0.125 to 0.125
- w_up: bfloat16 [64, 2048, 1408], P(('dp', 'expert'), None, 'tensor'), may hold values from -0.125 to 0.125
- w_down: bfloat16 [64, 1408, 2048], P(('dp', 'expert'), 'tensor'), may hold values from -0.15625 to 0.15625
Outputs:
- grad_tokens: bfloat16 [8192, 2048], P(('dp', 'expert', 'tensor'))
- grad_gate: bfloat16 [8192, 6], P(('dp', 'expert', 'tensor'))
- grad_down: float32 [64, 1408, 2048], P(('dp', 'expert'), 'tensor')
Inputs may be any that keep to these rules, and one draw needn't show every extreme that they name: `routes`: each row names 6 different experts. In each device's block of 32 rows no expert is named more than 4 times, and in some block an expert is named exactly 4 times.
All inputs are finite; a program needn't handle non-finite values.
Results may differ from a plain program's by a relative error of at most 0.0057.
Values may be sent and summed in bfloat16 or wider, within the bound.
A program may use at most 128 MiB of HBM per device.

v0:
```python
import jax
import jax.numpy as jnp
from jax import lax
from jax.sharding import PartitionSpec as P


def expert_ranks(picks, experts):
    onehot = (picks[..., None] == jnp.arange(experts, dtype=jnp.int32)).astype(jnp.int32)
    running = jnp.cumsum(onehot, axis=-2) - 1
    return jnp.sum(onehot * running, axis=-1)


def with_zero_row(values):
    filler = jnp.zeros((1,) + values.shape[1:], values.dtype)
    return jnp.concatenate([values, filler], axis=0)


def body(tokens, out_grad, routes, gates, w_gate, w_up, w_down):
    local_exp = w_gate.shape[0]
    width = tokens.shape[1]
    n_src = lax.axis_size(("dp", "expert"))
    experts = local_exp * n_src
    tok_count = tokens.shape[0]
    top_count = routes.shape[1]
    assign = tok_count * top_count
    capacity = max(2, min(tok_count, 4 * tok_count * top_count // (3 * experts)))
    own_picks = routes.reshape(assign)
    own_ranks = expert_ranks(own_picks, experts)
    own_owner = own_picks // local_exp
    own_local = own_picks % local_exp
    positions = (own_owner * local_exp + own_local) * capacity + own_ranks
    table = jnp.full((n_src * local_exp * capacity,), assign, jnp.int32)
    table = table.at[positions].set(jnp.arange(assign, dtype=jnp.int32))
    token_ids = table // top_count
    send_x = with_zero_row(tokens)[token_ids].reshape(n_src, local_exp, capacity, width)
    send_dy = with_zero_row(out_grad)[token_ids].reshape(n_src, local_exp, capacity, width)
    send_g = with_zero_row(gates.reshape(assign))[table].reshape(n_src, local_exp, capacity)
    recv_x, recv_dy, recv_g = (
        lax.all_to_all(send_x, ("dp", "expert"), split_axis=0, concat_axis=2, tiled=True),
        lax.all_to_all(send_dy, ("dp", "expert"), split_axis=0, concat_axis=2, tiled=True),
        lax.all_to_all(send_g, ("dp", "expert"), split_axis=0, concat_axis=2, tiled=True),
    )
    rows_x = recv_x.reshape(local_exp, n_src * capacity, width)
    rows_dy = recv_dy.reshape(local_exp, n_src * capacity, width)
    rows_g = recv_g.reshape(local_exp, n_src * capacity)
    part_x = lax.all_gather(rows_x, "tensor", axis=1, tiled=True)
    part_dy = lax.all_gather(rows_dy, "tensor", axis=1, tiled=True)
    part_g = lax.all_gather(rows_g, "tensor", axis=1, tiled=True)
    pre_gate = jnp.einsum("erd,edf->erf", part_x, w_gate, preferred_element_type=jnp.float32)
    pre_up = jnp.einsum("erd,edf->erf", part_x, w_up, preferred_element_type=jnp.float32)
    back_h = jnp.einsum("erd,efd->erf", part_dy, w_down, preferred_element_type=jnp.float32)
    sig = jax.nn.sigmoid(pre_gate)
    act = pre_gate * sig
    hidden = act * pre_up
    gate_f = part_g.astype(jnp.float32)[:, :, None]
    scaled = gate_f * back_h
    grad_pre_gate = (scaled * pre_up * sig * (1.0 + pre_gate * (1.0 - sig))).astype(jnp.bfloat16)
    grad_pre_up = (scaled * act).astype(jnp.bfloat16)
    weighted = (gate_f * part_dy.astype(jnp.float32)).astype(jnp.bfloat16)
    grads = jnp.einsum(
        "erf,erd->efd", hidden.astype(jnp.bfloat16), weighted, preferred_element_type=jnp.float32
    )
    gate_part = jnp.sum(hidden * back_h, axis=2).T
    grads, grad_a, grad_b, gate_part = (grads, grad_pre_gate, grad_pre_up, gate_part)
    mine_rows = lax.psum_scatter(
        jnp.einsum("erf,edf->red", grad_a, w_gate, preferred_element_type=jnp.float32)
        + jnp.einsum("erf,edf->red", grad_b, w_up, preferred_element_type=jnp.float32),
        "tensor",
        scatter_dimension=0,
        tiled=True,
    ).astype(jnp.bfloat16)
    mine_gate = lax.psum_scatter(gate_part, "tensor", scatter_dimension=0, tiled=True).astype(
        jnp.bfloat16
    )
    back_rows, back_gate = (
        lax.all_to_all(
            mine_rows.reshape(n_src, capacity, local_exp, width),
            ("dp", "expert"),
            split_axis=0,
            concat_axis=0,
            tiled=True,
        ),
        lax.all_to_all(
            mine_gate.reshape(n_src, capacity, local_exp),
            ("dp", "expert"),
            split_axis=0,
            concat_axis=0,
            tiled=True,
        ),
    )
    index = (own_owner * capacity + own_ranks) * local_exp + own_local
    picked_rows = back_rows.reshape(-1, width)[index].reshape(tok_count, top_count, width)
    grad_tokens = jnp.sum(picked_rows.astype(jnp.float32), axis=1).astype(jnp.bfloat16)
    grad_gate = back_gate.reshape(-1)[index].reshape(tok_count, top_count)
    return (grad_tokens, grad_gate, grads)


def solution(mesh):
    return jax.shard_map(
        body,
        mesh=mesh,
        in_specs=(
            P(("dp", "expert", "tensor"), None),
            P(("dp", "expert", "tensor"), None),
            P(("dp", "expert", "tensor"), None),
            P(("dp", "expert", "tensor"), None),
            P(("dp", "expert"), None, "tensor"),
            P(("dp", "expert"), None, "tensor"),
            P(("dp", "expert"), "tensor", None),
        ),
        out_specs=(
            P(("dp", "expert", "tensor"), None),
            P(("dp", "expert", "tensor"), None),
            P(("dp", "expert"), "tensor", None),
        ),
        check_vma=False,
    )
```

profile of v0, /device:TPU:1, one launch (start us, length us, event | category | flops | bytes accessed | tf_op | source)
XLA Modules:
  0.0 328.9 jit_solution(10537712245333023799)
XLA Ops:
  7.2 0.0 copy-start
  7.2 0.0 all-gather.5.cloned.1.call-start
  7.2 0.8 broadcast_multiply_fusion
  8.0 0.8 copy.18
  8.8 0.1 copy.17
  8.9 0.1 mul.74
  9.0 0.1 eq.24
  9.1 0.6 reduce-window.6
  9.7 0.2 slice_reduce_fusion
  10.0 0.1 bitcast_bitcast_fusion
  10.1 1.2 scatter_custom_fusion
  11.4 0.9 concatenate.11
  12.3 1.4 gather_fusion.2
  13.6 1.2 reshape.179
  14.9 40.7 %all_to_all.37 = bf16[64,1,4,2048]{3,2,1,0:T(4,128)(2,1)S(1)} all-to-all(bf16[64,1,4,2048]{3,2,1,0:T(4,128)(2,1)} %bitcast.64), channel_id=1, replica_groups=mesh['dp'=16,'expert'=4,'tensor'=4] {'dp','expert'}, dimensions={0} | all-to-all | bytes 2097152 | tf_op jit(solution)/shard_map/all_to_all | solution.py:39
  55.6 1.1 reshape.180
  56.7 0.0 all-gather.5.cloned.1.call-update
  56.7 0.0 all-gather.3.cloned.1.call-start
  56.8 1.4 gather_fusion.1
  58.1 0.4 reshape.175
  58.6 34.0 %all_to_all.38 = bf16[64,1,4,2048]{3,2,1,0:T(4,128)(2,1)S(1)} all-to-all(bf16[64,1,4,2048]{3,2,1,0:T(4,128)(2,1)S(1)} %bitcast.65), channel_id=1, replica_groups=mesh['dp'=16,'expert'=4,'tensor'=4] {'dp','expert'}, dimensions={0} | all-to-all | bytes 2097152 | tf_op jit(solution)/shard_map/all_to_all | solution.py:40
  92.6 1.2 reshape.176
  93.8 0.0 all-gather.3.cloned.1.call-update
  93.8 0.0 reduce-scatter.7.cloned.1.call-start
  93.9 0.1 copy.16
  94.0 0.1 reshape.170
  94.1 0.1 pad_maximum_fusion
  94.2 1.9 gather_fusion
  96.0 0.1 reshape.244
  96.2 15.4 %all_to_all.39 = bf16[64,1,4]{2,1,0:T(2,128)(2,1)S(1)} all-to-all(bf16[64,1,4]{2,1,0:T(2,128)(2,1)S(1)} %reshape.244), channel_id=1, replica_groups=mesh['dp'=16,'expert'=4,'tensor'=4] {'dp','expert'}, dimensions={0} | all-to-all | bytes 1024 | tf_op jit(solution)/shard_map/all_to_all | solution.py:41
  111.6 0.1 reduce.4
  111.7 0.1 reshape.174
  111.8 8.1 %all_gather.9 = bf16[1,1024]{1,0:T(2,128)(2,1)S(1)} all-gather(bf16[1,256]{1,0:T(2,128)(2,1)S(1)} %reshape.174), channel_id=1, replica_groups=mesh['dp'=16,'expert'=4,'tensor'=4] {'tensor'}, dimensions={1}, use_global_device_ids=true | all-gather | bytes 2560 | tf_op jit(solution)/shard_map/all_gather | solution.py:48
  120.0 4.3 %fusion.3 = f32[1024,352]{0,1:T(8,128)S(1)} fusion(bf16[1,1024,2048]{2,1,0:T(8,128)(2,1)} %all-gather.5.cloned.1.call-done, bf16[1,2048,352]{1,2,0:T(8,128)(2,1)S(1)} %copy-done), kind=kOutput, calls=%fused_computation.10 | convolution fusion | flops 1476395008 | bytes 7077888 | tf_op jit(solution)/shard_map/erd,edf->erf/dot_general | solution.py:49
  124.3 2.8 fusion.5
  127.1 30.9 %all-gather.3.cloned.1.call-done = bf16[1,1024,2048]{2,1,0:T(8,128)(2,1)} async-done(((bf16[1,256,2048]{2,1,0:T(8,128)(2,1)}), bf16[1,1024,2048]{2,1,0:T(8,128)(2,1)}) %all-gather.3.cloned.1.call-update) | async-done | bytes 4194320 | tf_op jit(solution)/shard_map/all_gather | solution.py:47
  158.0 5.9 %multiply_reduce_fusion = (f32[1024]{0:T(1024)S(1)}, f32[1024,352]{0,1:T(8,128)}) fusion(f32[1024,352]{0,1:T(8,128)} %fusion.5, f32[1024,352]{0,1:T(8,128)S(1)} %fusion.3, bf16[1,352,2048]{2,1,0:T(8,128)(2,1)} %param.13, bf16[1,1024,2048]{2,1,0:T(8,128)(2,1)} %all-gather.3.cloned.1.call-done), kind=kOutput, calls=%fused_computation.24 | convolution fusion | flops 1478917120 | bytes 9965568 | tf_op jit(solution)/shard_map/erd,efd->erf/dot_general | solution.py:51
  163.9 1.0 copy.27
  164.9 0.0 reduce-scatter.7.cloned.1.call-update
  165.0 0.0 reduce-scatter.5.cloned.1.call-start
  165.0 0.0 copy-start.1
  165.0 0.0 copy-start.3
  165.0 4.6 %fusion.13 = f32[1024,2048]{1,0:T(8,128)S(1)} fusion(bf16[1,2048,352]{1,2,0:T(8,128)(2,1)S(1)} %copy-done, f32[1024,352]{0,1:T(8,128)S(1)} %fusion.3, f32[1024,352]{0,1:T(8,128)} %fusion.5, f32[1024,352]{0,1:T(8,128)} %get-tuple-element.12, f32[1024]{0:T(1024)S(1)} %bitcast.66), kind=kOutput, calls=%fused_computation.18 | convolution fusion | flops 1480359936 | bytes 14159872 | tf_op jit(solution)/shard_map/erf,edf->red/dot_general | solution.py:66
  169.7 5.9 %add_bitcast_fusion = f32[1024,1,2048]{2,0,1:T(8,128)} fusion(f32[1024,2048]{1,0:T(8,128)S(1)} %fusion.13, bf16[1,2048,352]{1,2,0:T(8,128)(2,1)S(1)} %copy-done.3, f32[1024,352]{0,1:T(8,128)S(1)} %copy-done.1, f32[1024]{0:T(1024)S(1)} %bitcast.67, f32[1024,352]{0,1:T(8,128)S(1)} %fusion.3), kind=kOutput, calls=%fused_computation.7 | convolution fusion | flops 1481015296 | bytes 21106688 | tf_op jit(solution)/shard_map/erf,edf->red/dot_general | solution.py:67
  175.6 0.0 reduce-scatter.5.cloned.1.call-update
  175.6 12.2 %reduce-scatter.7.cloned.1.call-done = f32[256,1]{1,0:T(8,128)} async-done(((f32[1024,1]{1,0:T(8,128)}), f32[256,1]{1,0:T(8,128)}) %reduce-scatter.7.cloned.1.call-update) | async-done | bytes 1040
  187.8 1.0 copy.28
  188.8 0.8 reshape.245
  189.6 12.3 %all-to-all-start.4 = ((bf16[64,4,1]{1,2,0:T(2,128)(2,1)}), bf16[64,4,1]{1,2,0:T(2,128)(2,1)S(1)}, u32[]{:S(2)}, u32[]{:S(2)}) async-start(bf16[64,4,1]{1,2,0:T(2,128)(2,1)} %reshape.245), calls=%async_computation.5 | async-start | bytes 65536 | tf_op jit(solution)/shard_map/all_to_all | solution.py:83
  201.9 73.0 %reduce-scatter.5.cloned.1.call-done = f32[256,1,2048]{2,0,1:T(8,128)} async-done(((f32[1024,1,2048]{2,0,1:T(8,128)}), f32[256,1,2048]{2,0,1:T(8,128)}) %reduce-scatter.5.cloned.1.call-update) | async-done | bytes 2097168 | tf_op jit(solution)/shard_map/reduce_scatter | solution.py:65
  274.8 2.7 convert_element_type.31
  277.5 2.2 reshape.184
  279.8 10.8 %all-to-all-start.3 = ((bf16[64,4,1,2048]{3,1,2,0:T(4,128)(2,1)}), bf16[64,4,1,2048]{3,1,2,0:T(4,128)(2,1)}, u32[]{:S(2)}, u32[]{:S(2)}) async-start(bf16[64,4,1,2048]{3,1,2,0:T(4,128)(2,1)} %bitcast.63), calls=%async_computation.4 | async-start | bytes 2097152 | tf_op jit(solution)/shard_map/all_to_all | solution.py:76
  290.6 6.1 %fusion.10 = f32[1,352,2048]{2,1,0:T(8,128)} fusion(bf16[1,1024,2048]{2,1,0:T(8,128)(2,1)} %all-gather.3.cloned.1.call-done, f32[1024]{0:T(1024)S(1)} %bitcast.68, f32[1024,352]{0,1:T(8,128)} %fusion.5, f32[1024,352]{0,1:T(8,128)S(1)} %fusion.3), kind=kOutput, calls=%fused_computation.17 | convolution fusion | flops 1484849152 | bytes 9965568 | tf_op jit(solution)/shard_map/erf,erd->efd/dot_general | solution.py:60
  296.7 0.1 reduce.6
  296.8 0.1 reshape.188
  296.9 1.6 gather_fusion.4
  298.5 0.1 reshape.189
  298.6 0.7 copy.26
  299.3 19.0 %all-to-all-done.3 = bf16[64,4,1,2048]{3,1,2,0:T(4,128)(2,1)} async-done(((bf16[64,4,1,2048]{3,1,2,0:T(4,128)(2,1)}), bf16[64,4,1,2048]{3,1,2,0:T(4,128)(2,1)}, u32[]{:S(2)}, u32[]{:S(2)}) %all-to-all-start.3) | async-done | bytes 1048608 | tf_op jit(solution)/shard_map/all_to_all | solution.py:76
  318.2 1.3 reshape.185
  319.6 1.1 gather_fusion.3
  320.7 0.3 reshape.186
  321.0 1.4 reduce_sum.34
  (26 shorter events, 0.2 us)
Async XLA Ops:
  7.2 112.8 %copy-start = (bf16[1,2048,352]{1,2,0:T(8,128)(2,1)S(1)}, bf16[1,2048,352]{1,2,0:T(8,128)(2,1)}, u32[]{:S(2)}) copy-start(bf16[1,2048,352]{1,2,0:T(8,128)(2,1)} %param.11) | copy-start | bytes 4325380
  7.2 112.8 %all-gather.5.cloned.1.call-start = ((), (), s32[]{:S(2)}) async-start(), calls=%async_computation.8 | async-start | bytes 5242880 | tf_op jit(solution)/shard_map/all_gather | solution.py:46
  55.6 1.2 copy-start.4
  56.7 101.3 %all-gather.3.cloned.1.call-start = ((), (), s32[]{:S(2)}) async-start(), calls=%async_computation.7 | async-start | bytes 5242880 | tf_op jit(solution)/shard_map/all_gather | solution.py:47
  92.6 1.3 copy-start.5
  93.8 94.0 %reduce-scatter.7.cloned.1.call-start = ((), (), s32[]{:S(2)}) async-start(), calls=%async_computation.10 | async-start | bytes 655360
  120.0 4.3 %copy-start.2 = (bf16[1,2048,352]{1,2,0:T(8,128)(2,1)S(1)}, bf16[1,2048,352]{1,2,0:T(8,128)(2,1)}, u32[]{:S(2)}) copy-start(bf16[1,2048,352]{1,2,0:T(8,128)(2,1)} %param.12) | copy-start | bytes 4325380
  120.0 4.3 %copy-start.6 = (bf16[1,1024,2048]{2,1,0:T(8,128)(2,1)S(1)}, bf16[1,1024,2048]{2,1,0:T(8,128)(2,1)}, u32[]{:S(2)}) copy-start(bf16[1,1024,2048]{2,1,0:T(8,128)(2,1)} %all-gather.5.cloned.1.call-done) | copy-start | bytes 12582916
  165.0 109.9 %reduce-scatter.5.cloned.1.call-start = ((), (), s32[]{:S(2)}) async-start(), calls=%async_computation.9 | async-start | bytes 10485760 | tf_op jit(solution)/shard_map/reduce_scatter | solution.py:65
  165.0 4.7 %copy-start.1 = (f32[1024,352]{0,1:T(8,128)S(1)}, f32[1024,352]{0,1:T(8,128)}, u32[]{:S(2)}) copy-start(f32[1024,352]{0,1:T(8,128)} %get-tuple-element.12) | copy-start | bytes 4325380
  165.0 4.7 %copy-start.3 = (bf16[1,2048,352]{1,2,0:T(8,128)(2,1)S(1)}, bf16[1,2048,352]{1,2,0:T(8,128)(2,1)}, u32[]{:S(2)}) copy-start(bf16[1,2048,352]{1,2,0:T(8,128)(2,1)} %param.12) | copy-start | bytes 4325380
  189.6 90.2 %all-to-all-start.4 = ((bf16[64,4,1]{1,2,0:T(2,128)(2,1)}), bf16[64,4,1]{1,2,0:T(2,128)(2,1)S(1)}, u32[]{:S(2)}, u32[]{:S(2)}) async-start(bf16[64,4,1]{1,2,0:T(2,128)(2,1)} %reshape.245), calls=%async_computation.5 | async-start | bytes 65536 | tf_op jit(solution)/shard_map/all_to_all | solution.py:83
  279.8 38.5 %all-to-all-start.3 = ((bf16[64,4,1,2048]{3,1,2,0:T(4,128)(2,1)}), bf16[64,4,1,2048]{3,1,2,0:T(4,128)(2,1)}, u32[]{:S(2)}, u32[]{:S(2)}) async-start(bf16[64,4,1,2048]{3,1,2,0:T(4,128)(2,1)} %bitcast.63), calls=%async_computation.4 | async-start | bytes 2097152 | tf_op jit(solution)/shard_map/all_to_all | solution.py:76
Sparse Core Ops, SparseCore 0:
  56.8 48.1 all-gather.4
  106.8 51.1 all-gather.2
  165.1 22.6 reduce-scatter.6
  190.3 84.5 reduce-scatter.4
where the time goes:
time: 330 us; the launch traced here: 329 us
  waiting for transfers between devices  135 us (41%)
  blocking collectives  98.3 us (30%)
  matrix products  29.7 us (9%)
  starting transfers between devices  23.2 us (7%)
  local copies, waits for them, and re-layouts  22.6 us (7%)
  between operations  14.1 us (4%)
  other arithmetic  5.97 us (2%)
    reduce_scatter x1, waiting for transfers between devices, body(): lax.psum_scatter(jnp.einsum('erf,edf->red', grad_a, w_gate, preferred_ele...  73 us
    all_to_all x1, blocking collectives, body(): lax.all_to_all(send_x, ('dp', 'expert'), split_axis=0, concat_axis=2, til...  40.7 us
    all_to_all x1, blocking collectives, body(): lax.all_to_all(send_dy, ('dp', 'expert'), split_axis=0, concat_axis=2, ti...  34 us
    all_gather x1, waiting for transfers between devices, body(): part_dy = lax.all_gather(rows_dy, 'tensor', axis=1, tiled=True)  30.9 us
    all_to_all x1, waiting for transfers between devices, body(): lax.all_to_all(mine_rows.reshape(n_src, capacity, local_exp, width), ('dp...  19 us
    all_to_all x1, blocking collectives, body(): lax.all_to_all(send_g, ('dp', 'expert'), split_axis=0, concat_axis=2, til...  15.4 us
    all_to_all x1, starting transfers between devices, body(): lax.all_to_all(mine_gate.reshape(n_src, capacity, local_exp), ('dp', 'exp...  12.3 us
    unnamed x5, waiting for transfers between devices  12.2 us
  transfers between devices with their start and end apart: 6, of which 4 were waited for; matrix products, arithmetic and copies ran while one was open for 12% of the time, Pallas kernels for 0%

commit v1 on v0

v1 whole, which is shorter than its diff:
```python
import dataclasses
import functools

import jax
import jax.numpy as jnp
from jax import lax
from jax.experimental import pallas as pl
from jax.experimental.pallas import tpu as pltpu
from jax.sharding import PartitionSpec as P

MESH = pl.DeviceIdType.MESH
F32 = jnp.float32
BF16 = jnp.bfloat16
LANES = 128
CW = 3 * LANES


@dataclasses.dataclass(frozen=True)
class Sizes:
    n_dp: int
    n_x: int
    tok: int
    top: int
    cap: int
    width: int
    ff: int

    @property
    def rows(self):
        return self.n_dp * self.n_x * self.cap

    @property
    def mix(self):
        return self.width // CW

    @property
    def fwd(self):
        return 2 * self.mix + 1

    @property
    def ret(self):
        return self.mix + 1


def dot_nn(a, b):
    return lax.dot_general(a, b, (((1,), (0,)), ((), ())), preferred_element_type=F32)


def dot_nt(a, b):
    return lax.dot_general(a, b, (((1,), (1,)), ((), ())), preferred_element_type=F32)


def onehot(cond):
    return jnp.where(cond, 1.0, 0.0).astype(BF16)


def log2(n):
    assert n & (n - 1) == 0
    return n.bit_length() - 1


def kernel(
    z, routes_ref, gates_ref, tok_ref, dy_ref, wg_hbm, wu_hbm, wd_hbm,
    out_tok, out_gate, out_down,
    xc, sel, rx, sd, g, wg, wu, wd0, wd, pg, pu, hf, ht, bh, gt, gg, gu, gp, mats, pt,
    os_, ora, orb, am, ap, arp, arm, rd, rb, sx, hb,
    w_sem, xs, xr, ds_, dr, ys, yra, yrb, yrc, yrd,
    os_s, ora_r, orb_r, a_s, arp_r, arm_r, rd_s, rb_r, sx_s, hb_r,
):
    dp = lax.axis_index("dp")
    x = lax.axis_index("expert")
    y = lax.axis_index("tensor")
    rows, cap, n_dp, n_x, mix = z.rows, z.cap, z.n_dp, z.n_x, z.mix
    half = rows // 2
    xb, db = n_dp * cap, n_x * cap
    up, down, far = lax.rem(y + 1, 4), lax.rem(y + 3, 4), lax.rem(y + 2, 4)
    dev_up, dev_down = (dp, x, up), (dp, x, down)

    def wcopy(i):
        if i == 0:
            return pltpu.make_async_copy(wg_hbm, wg.at[pl.ds(0, z.width)], w_sem.at[0])
        if i == 1:
            return pltpu.make_async_copy(wu_hbm, wu.at[pl.ds(0, z.width)], w_sem.at[1])
        if i == 2:
            return pltpu.make_async_copy(wd_hbm.at[:, pl.ds(0, LANES)], wd0, w_sem.at[2])
        j = i - 3
        return pltpu.make_async_copy(
            wd_hbm.at[:, pl.ds(LANES + j * CW, CW)], wd.at[j], w_sem.at[i]
        )

    for i in range(3 + mix):
        wcopy(i).start()

    barrier = pltpu.get_barrier_semaphore()

    def greet_dp(j, c):
        pl.semaphore_signal(
            barrier, inc=1, device_id=(lax.rem(dp + j, n_dp), x, y), device_id_type=MESH
        )
        return c

    def greet_x(j, c):
        pl.semaphore_signal(
            barrier, inc=1, device_id=(dp, lax.rem(x + j, n_x), y), device_id_type=MESH
        )
        return c

    lax.fori_loop(1, n_dp, greet_dp, 0)
    lax.fori_loop(1, n_x, greet_x, 0)
    pl.semaphore_signal(barrier, inc=1, device_id=dev_up, device_id_type=MESH)
    pl.semaphore_signal(barrier, inc=1, device_id=dev_down, device_id_type=MESH)

    slot = lax.broadcasted_iota(jnp.int32, (z.tok, rows), 1)
    s_x = slot >> log2(xb)
    s_dp = (slot & (xb - 1)) >> log2(cap)
    s_rank = slot & (cap - 1)
    s_e = s_dp * n_x + s_x
    named = jnp.zeros((z.tok, rows), F32)
    gate = jnp.zeros((z.tok, rows), F32)
    for k in range(z.top):
        hit = routes_ref[:, k : k + 1] == s_e
        named = jnp.where(hit, 1.0, named)
        gate = jnp.where(hit, gates_ref[:, k : k + 1].astype(F32), gate)
    t_row = lax.broadcasted_iota(jnp.int32, (z.tok, z.tok), 0)
    t_col = lax.broadcasted_iota(jnp.int32, (z.tok, z.tok), 1)
    rank = dot_nn(onehot(t_col < t_row), named.astype(BF16))
    picked = jnp.where(rank == s_rank.astype(F32), named, 0.0)
    pt[...] = picked.astype(BF16)
    i_row = lax.broadcasted_iota(jnp.int32, (rows, rows), 0)
    i_col = lax.broadcasted_iota(jnp.int32, (rows, rows), 1)
    eye = onehot(i_row == i_col)
    place = dot_nt(eye, picked.astype(BF16)).astype(BF16)
    place_gate = dot_nt(eye, (picked * gate).astype(BF16)).astype(BF16)
    def reordered(i):
        return (
            ((i & (db - 1)) >> log2(cap)) * xb + (i >> log2(db)) * cap + (i & (cap - 1))
        )

    mats[0] = onehot(i_col == reordered(i_row))
    mats[1] = onehot(i_row == reordered(i_col))

    for q in range(mix):
        xc[q] = tok_ref[:, q * CW : (q + 1) * CW]
        xc[mix + 1 + q] = dy_ref[:, LANES + q * CW : LANES + (q + 1) * CW]
    xc[mix, :, 0:LANES] = tok_ref[:, mix * CW :]
    xc[mix, :, LANES : 2 * LANES] = jnp.zeros((z.tok, LANES), BF16)
    xc[mix, :, 2 * LANES :] = dy_ref[:, 0:LANES]

    def choose(q, c):
        sel[q] = dot_nn(place, xc[q]).astype(BF16)
        return c

    lax.fori_loop(0, z.fwd, choose, 0)
    sel[mix, :, LANES : 2 * LANES] = dot_nn(
        place_gate, jnp.ones((z.tok, LANES), BF16)
    ).astype(BF16)

    def clear(o, c):
        pg[o] = jnp.zeros((rows, z.ff), F32)
        pu[o] = jnp.zeros((rows, z.ff), F32)
        return c

    lax.fori_loop(0, 4, clear, 0)
    wg[pl.ds(z.width, 2 * LANES)] = jnp.zeros((2 * LANES, z.ff), BF16)
    wu[pl.ds(z.width, 2 * LANES)] = jnp.zeros((2 * LANES, z.ff), BF16)

    pl.semaphore_wait(barrier, n_dp - 1 + n_x - 1 + 2)

    def remote(src, dst, send, recv, dev):
        return pltpu.make_async_remote_copy(
            src_ref=src, dst_ref=dst, send_sem=send, recv_sem=recv,
            device_id=dev, device_id_type=MESH,
        )

    def got(region, sem):
        remote(region, region, sem, sem, dev_up).wait_recv()

    def left(region, sem):
        remote(region, region, sem, sem, dev_up).wait_send()

    def f0(q):
        rx[q, pl.ds(pl.multiple_of(x * xb, 16), xb)] = sel[q, pl.ds(pl.multiple_of(x * xb, 16), xb)]

        def send(j, c):
            to = lax.rem(x + j, n_x)
            remote(
                sel.at[q, pl.ds(pl.multiple_of(to * xb, 16), xb)],
                rx.at[q, pl.ds(pl.multiple_of(x * xb, 16), xb)],
                xs.at[q], xr.at[q], (dp, to, y),
            ).start()
            return c

        lax.fori_loop(1, n_x, send, 0)

    def f1(q):
        got(rx.at[q, pl.ds(0, rows - xb)], xr.at[q])
        sd[q] = dot_nn(mats[0], rx[q]).astype(BF16)
        mine = pl.ds(pl.multiple_of(dp * db, 16), db)

        def send(j, c):
            to = lax.rem(dp + j, n_dp)
            remote(
                sd.at[q, pl.ds(pl.multiple_of(to * db, 16), db)],
                g.at[q, y, mine],
                ds_.at[q], dr.at[q], (to, x, y),
            ).start()
            return c

        lax.fori_loop(1, n_dp, send, 0)
        g[q, y, mine] = sd[q, mine]

    def f2(q):
        got(g.at[q, y, pl.ds(0, rows - db)], dr.at[q])
        remote(g.at[q, y], g.at[q, y], ys.at[q], yra.at[q], dev_up).start()
        remote(g.at[q, y], g.at[q, y], ys.at[q], yrb.at[q], dev_down).start()

    def f3(q):
        got(g.at[q, down], yra.at[q])
        first = g.at[q, down, pl.ds(0, half)]
        remote(first, first, ys.at[q], yrc.at[q], dev_up).start()
        got(g.at[q, up], yrb.at[q])
        second = g.at[q, up, pl.ds(half, half)]
        remote(second, second, ys.at[q], yrd.at[q], dev_down).start()

    def f4(q):
        got(g.at[q, far, pl.ds(0, half)], yrc.at[q])
        got(g.at[q, far, pl.ds(half, half)], yrd.at[q])

        @pl.when(q < mix)
        def _():
            part = pl.ds(pl.multiple_of(q * CW, LANES), CW)

            def one(o, c):
                pg[o] += dot_nn(g[q, o], wg[part])
                pu[o] += dot_nn(g[q, o], wu[part])
                return c

            lax.fori_loop(0, 4, one, 0)

        @pl.when(q == mix)
        def _():
            def one(o, down_acc):
                xe = g[q, o, :, 0:LANES]
                tail = pl.ds(mix * CW, LANES)
                pre_gate = pg[o] + dot_nn(xe, wg[tail])
                pre_up = pu[o] + dot_nn(xe, wu[tail])
                sig = 1.0 / (1.0 + jnp.exp(-pre_gate))
                act = pre_gate * sig
                hidden = act * pre_up
                pg[o] = act
                pu[o] = pre_up * sig * (1.0 + pre_gate * (1.0 - sig))
                hf[o] = hidden
                r = lax.broadcasted_iota(jnp.int32, (z.ff, z.ff), 0)
                c = lax.broadcasted_iota(jnp.int32, (z.ff, z.ff), 1)
                ht[o] = dot_nt(onehot(r == c), hidden.astype(BF16)).astype(BF16)
                gt[o] = g[q, o, :, LANES : 2 * LANES].astype(F32)
                dye = g[q, o, :, 2 * LANES : 3 * LANES]
                bh[o] = dot_nt(dye, wd0[...])
                weighted = (gt[o] * dye.astype(F32)).astype(BF16)
                return down_acc + dot_nn(ht[o], weighted)

            out_down[:, 0:LANES] = lax.fori_loop(0, 4, one, jnp.zeros((z.ff, LANES), F32))

        @pl.when(q > mix)
        def _():
            j = q - mix - 1
            cols = pl.ds(pl.multiple_of(LANES + j * CW, LANES), CW)
            out_down[:, cols] = jnp.zeros((z.ff, CW), F32)

            def one(o, c):
                dye = g[q, o]
                bh[o] += dot_nt(dye, wd[j])
                scale = jnp.concatenate([gt[o]] * 3, axis=1)
                weighted = (scale * dye.astype(F32)).astype(BF16)
                out_down[:, cols] += dot_nn(ht[o], weighted)
                return c

            lax.fori_loop(0, 4, one, 0)

    def at(t, n, do):
        pl.when(jnp.logical_and(t >= 0, t < n))(functools.partial(do, t))

    for i in range(3 + mix):
        wcopy(i).wait()

    def tick_out(t, c):
        at(t - 2, z.fwd, f2)
        at(t - 3, z.fwd, f3)
        at(t - 1, z.fwd, f1)
        at(t, z.fwd, f0)
        at(t - 4, z.fwd, f4)
        return c

    lax.fori_loop(0, z.fwd + 4, tick_out, 0)

    def middle(o, c):
        back_h = bh[o]
        scaled = gt[o][:, 0:1] * back_h
        gg[o] = (scaled * pu[o]).astype(BF16)
        gu[o] = (scaled * pg[o]).astype(BF16)
        gp[o] = jnp.broadcast_to(
            jnp.sum(hf[o] * back_h, axis=1, keepdims=True), (rows, LANES)
        )
        return c

    lax.fori_loop(0, 4, middle, 0)

    def partial_rows(o, r):
        part = pl.ds(pl.multiple_of(r * CW, LANES), CW)
        total = dot_nt(gg[o], wg[part]) + dot_nt(gu[o], wu[part])
        lane = lax.broadcasted_iota(jnp.int32, (rows, CW), 1)
        at_gate = jnp.logical_and(lane >= LANES, lane < 2 * LANES)
        extra = jnp.where(at_gate, gp[o][:, 0:1], 0.0)
        return total + jnp.where(r == mix, 1.0, 0.0) * extra

    lo, hi = pl.ds(0, half), pl.ds(half, half)

    def r0(r):
        os_[r] = partial_rows(far, r).astype(BF16)
        remote(os_.at[r, lo], ora.at[r], os_s.at[r], ora_r.at[r], dev_down).start()
        remote(os_.at[r, hi], orb.at[r], os_s.at[r], orb_r.at[r], dev_up).start()

    def r1(r):
        mine = partial_rows(down, r)
        got(ora.at[r], ora_r.at[r])
        am[r, lo] = (mine[0:half] + ora[r].astype(F32)).astype(BF16)
        am[r, hi] = mine[half:].astype(BF16)
        remote(am.at[r], arp.at[r], a_s.at[r], arp_r.at[r], dev_down).start()
        mine = partial_rows(up, r)
        got(orb.at[r], orb_r.at[r])
        ap[r, lo] = mine[0:half].astype(BF16)
        ap[r, hi] = (mine[half:] + orb[r].astype(F32)).astype(BF16)
        remote(ap.at[r], arm.at[r], a_s.at[r], arm_r.at[r], dev_up).start()

    def r2(r):
        mine = partial_rows(y, r)
        got(arp.at[r], arp_r.at[r])
        got(arm.at[r], arm_r.at[r])
        rd[r] = (mine + arp[r].astype(F32) + arm[r].astype(F32)).astype(BF16)
        own = pl.ds(pl.multiple_of(dp * db, 16), db)

        def send(j, c):
            to = lax.rem(dp + j, n_dp)
            remote(
                rd.at[r, pl.ds(pl.multiple_of(to * db, 16), db)], rb.at[r, own],
                rd_s.at[r], rb_r.at[r], (to, x, y),
            ).start()
            return c

        lax.fori_loop(1, n_dp, send, 0)
        rb[r, own] = rd[r, own]

    def r3(r):
        got(rb.at[r, pl.ds(0, rows - db)], rb_r.at[r])
        sx[r] = dot_nn(mats[1], rb[r]).astype(BF16)
        own = pl.ds(pl.multiple_of(x * xb, 16), xb)

        def send(j, c):
            to = lax.rem(x + j, n_x)
            remote(
                sx.at[r, pl.ds(pl.multiple_of(to * xb, 16), xb)], hb.at[r, own],
                sx_s.at[r], hb_r.at[r], (dp, to, y),
            ).start()
            return c

        lax.fori_loop(1, n_x, send, 0)
        hb[r, own] = sx[r, own]

    def r4(r):
        got(hb.at[r, pl.ds(0, rows - xb)], hb_r.at[r])

        @pl.when(r < mix)
        def _():
            cols = pl.ds(pl.multiple_of(r * CW, LANES), CW)
            out_tok[:, cols] = dot_nn(pt[...], hb[r]).astype(BF16)

        @pl.when(r == mix)
        def _():
            out_tok[:, mix * CW :] = dot_nn(pt[...], hb[r, :, 0:LANES]).astype(BF16)
            row = lax.broadcasted_iota(jnp.int32, (rows, LANES), 0)
            lane = lax.broadcasted_iota(jnp.int32, (rows, LANES), 1)
            e = ((row & (xb - 1)) >> log2(cap)) * n_x + (row >> log2(xb))
            vals = jnp.where(e == lane, hb[r, :, LANES : 2 * LANES].astype(F32), 0.0)
            by_expert = dot_nn(pt[...], vals.astype(BF16))
            lane_t = lax.broadcasted_iota(jnp.int32, (z.tok, LANES), 1)
            for k in range(z.top):
                hit = routes_ref[:, k : k + 1] == lane_t
                out_gate[:, k : k + 1] = jnp.sum(
                    jnp.where(hit, by_expert, 0.0), axis=1, keepdims=True
                ).astype(BF16)

    def tick_back(t, c):
        at(t, z.ret, r0)
        at(t - 1, z.ret, r1)
        at(t - 2, z.ret, r2)
        at(t - 3, z.ret, r3)
        at(t - 4, z.ret, r4)
        return c

    lax.fori_loop(0, z.ret + 4, tick_back, 0)

    def drain_out(q, c):
        left(sel.at[q, pl.ds(0, rows - xb)], xs.at[q])
        left(sd.at[q, pl.ds(0, rows - db)], ds_.at[q])
        left(g.at[q, pl.ds(0, 3)], ys.at[q])
        return c

    def drain_back(r, c):
        left(os_.at[r], os_s.at[r])
        left(g.at[r, pl.ds(0, 2)], a_s.at[r])
        left(rd.at[r, pl.ds(0, rows - db)], rd_s.at[r])
        left(sx.at[r, pl.ds(0, rows - xb)], sx_s.at[r])
        return c

    lax.fori_loop(0, z.fwd, drain_out, 0)
    lax.fori_loop(0, z.ret, drain_back, 0)


def body(cap, tokens, out_grad, routes, gates, w_gate, w_up, w_down):
    z = Sizes(
        n_dp=lax.axis_size("dp"), n_x=lax.axis_size("expert"), tok=tokens.shape[0],
        top=routes.shape[1], cap=cap, width=tokens.shape[1], ff=w_gate.shape[2],
    )
    assert lax.axis_size("tensor") == 4 and z.width % CW == LANES
    rows, half, fwd, ret, mix = z.rows, z.rows // 2, z.fwd, z.ret, z.mix
    vm = pltpu.VMEM
    sem = pltpu.SemaphoreType.DMA
    scratch = [
        vm((fwd, z.tok, CW), BF16),
        vm((fwd, rows, CW), BF16),
        vm((fwd, rows, CW), BF16),
        vm((fwd, rows, CW), BF16),
        vm((fwd, 4, rows, CW), BF16),
        vm((z.width + 2 * LANES, z.ff), BF16),
        vm((z.width + 2 * LANES, z.ff), BF16),
        vm((z.ff, LANES), BF16),
        vm((mix, z.ff, CW), BF16),
        vm((4, rows, z.ff), F32),
        vm((4, rows, z.ff), F32),
        vm((4, rows, z.ff), F32),
        vm((4, z.ff, rows), BF16),
        vm((4, rows, z.ff), F32),
        vm((4, rows, LANES), F32),
        vm((4, rows, z.ff), BF16),
        vm((4, rows, z.ff), BF16),
        vm((4, rows, LANES), F32),
        vm((2, rows, rows), BF16),
        vm((z.tok, rows), BF16),
        vm((ret, rows, CW), BF16),
        vm((ret, half, CW), BF16),
        vm((ret, half, CW), BF16),
        vm((ret, rows, CW), BF16),
        vm((ret, rows, CW), BF16),
        vm((ret, rows, CW), BF16),
        vm((ret, rows, CW), BF16),
        vm((ret, rows, CW), BF16),
        vm((ret, rows, CW), BF16),
        vm((ret, rows, CW), BF16),
        vm((ret, rows, CW), BF16),
        sem((3 + mix,)),
    ] + [sem((fwd,))] * 9 + [sem((ret,))] * 10
    vmem = pl.BlockSpec(memory_space=pltpu.VMEM)
    hbm = pl.BlockSpec(memory_space=pl.ANY)
    grad_tokens, grad_gate, grad_down = pl.pallas_call(
        functools.partial(kernel, z),
        out_shape=(
            jax.ShapeDtypeStruct((z.tok, z.width), BF16),
            jax.ShapeDtypeStruct((z.tok, z.top), BF16),
            jax.ShapeDtypeStruct((z.ff, z.width), F32),
        ),
        in_specs=[vmem] * 4 + [hbm] * 3,
        out_specs=(vmem, vmem, vmem),
        scratch_shapes=scratch,
        compiler_params=pltpu.CompilerParams(
            collective_id=0, has_side_effects=True, vmem_limit_bytes=60 * 1024 * 1024
        ),
    )(routes, gates, tokens, out_grad, w_gate[0], w_up[0], w_down[0])
    return grad_tokens, grad_gate, grad_down[None]


def solution(mesh, cap=4):
    tokens = P(("dp", "expert", "tensor"), None)
    return jax.shard_map(
        functools.partial(body, cap),
        mesh=mesh,
        in_specs=(
            tokens, tokens, tokens, tokens,
            P(("dp", "expert"), None, "tensor"),
            P(("dp", "expert"), None, "tensor"),
            P(("dp", "expert"), "tensor", None),
        ),
        out_specs=(tokens, tokens, P(("dp", "expert"), "tensor", None)),
        check_vma=False,
    )
```

time: 330 us -> 188 us (0.57)
  Pallas kernels: 0 us -> 174 us
  waiting for transfers between devices: 135 us -> 0 us
  blocking collectives: 98.3 us -> 0 us
  matrix products: 29.7 us -> 0 us
  starting transfers between devices: 23.2 us -> 0 us
  between operations: 14.1 us -> 0.65 us
  local copies, waits for them, and re-layouts: 22.6 us -> 13.6 us
  other arithmetic: 5.97 us -> 0 us
    pallas_call x0 -> x1, Pallas kernels: none -> 174 us  [body(): pl.pallas_call(functools.partial(kernel, z), out_shape=(jax.ShapeDtypeStr...]
    all_to_all x3 -> x0, blocking collectives: 90.2 us -> none  [the longest x1 40.7 us: body(): lax.all_to_all(send_x, ('dp', 'expert'), split_axis=0, concat_axis=2, til...]
    reduce_scatter x1 -> x0, waiting for transfers between devices: 73 us -> none  [body(): lax.psum_scatter(jnp.einsum('erf,edf->red', grad_a, w_gate, preferred_ele...]
    all_gather x2 -> x0, waiting for transfers between devices: 30.9 us -> none  [the longest x1 30.9 us: body(): part_dy = lax.all_gather(rows_dy, 'tensor', axis=1, tiled=True)]
    dot_general x6 -> x0, matrix products: 29.7 us -> none  [the longest x1 6.1 us: body(): jnp.einsum('erf,erd->efd', hidden.astype(jnp.bfloat16), weighted, preferr...]
    all_to_all x2 -> x0, starting transfers between devices: 23.1 us -> none  [the longest x1 12.3 us: body(): lax.all_to_all(mine_gate.reshape(n_src, capacity, local_exp), ('dp', 'exp...]
    all_to_all x2 -> x0, waiting for transfers between devices: 19 us -> none  [the longest x1 19 us: body(): lax.all_to_all(mine_rows.reshape(n_src, capacity, local_exp, width), ('dp...]
    unnamed x5 -> x0, waiting for transfers between devices: 12.2 us -> none
  transfers between devices with their start and end apart: 6 -> 0, of which waited for: 4 -> 0; matrix products, arithmetic and copies ran while one was open for 12% -> 0% of each run, Pallas kernels for 0% -> 0%
where the time goes in v1:
time: 188 us
  Pallas kernels  174 us (93%)
  local copies, waits for them, and re-layouts  13.6 us (7%)
    pallas_call x1, Pallas kernels, body(): pl.pallas_call(functools.partial(kernel, z), out_shape=(jax.ShapeDtypeStr...  174 us
    unnamed x9, local copies, waits for them, and re-layouts  13.6 us

profile of v1, /device:TPU:1, one launch (start us, length us, event | category | flops | bytes accessed | tf_op | source)
XLA Modules:
  0.0 187.8 jit_solution(14800834338205567268)
XLA Ops:
  0.6 0.0 copy-start
  0.6 1.5 copy.13.gates_ref
  2.1 1.4 copy.12.routes_ref
  3.5 2.6 %copy.10 = bf16[1,2048,352]{2,1,0:T(8,128)(2,1)} copy(bf16[1,2048,352]{1,2,0:T(8,128)(2,1)} %param.11) | data formatting | bytes 2883584 | tf_op args[4]
  6.0 0.0 copy-done
  6.0 1.6 copy.11
  7.6 173.5 %shard_map.94 = (bf16[32,2048]{1,0:T(8,128)(2,1)}, bf16[32,6]{1,0:T(8,128)(2,1)}, f32[352,2048]{1,0:T(8,128)}) custom-call(s32[32,6]{1,0:T(8,128)} %copy.12.routes_ref, bf16[32,6]{1,0:T(8,128)(2,1)} %copy.13.gates_ref, bf16[32,2048]{1,0:T(8,128)(2,1)} %tok_ref.1, bf16[32,2048]{1,0:T(8,128)(2,1)} %dy_ref.1, bf16[2048,352]{1,0:T(8,128)(2,1)} %bitcast.4, ...), custom_call_target="tpu_custom_call" | custom-call | tf_op jit(solution)/shard_map/pallas_call | solution.py:464
  181.1 1.4 copy.14
  182.5 1.6 copy.17
  184.1 3.7 %copy.18 = f32[1,352,2048]{2,1,0:T(8,128)} copy(f32[1,352,2048]{2,1,0:T(8,128)} %bitcast.6) | data formatting | bytes 5767168
Async XLA Ops:
  0.6 5.4 %copy-start = (bf16[1,2048,352]{1,2,0:T(8,128)(2,1)S(1)}, bf16[1,2048,352]{1,2,0:T(8,128)(2,1)}, u32[]{:S(2)}) copy-start(bf16[1,2048,352]{1,2,0:T(8,128)(2,1)} %param.12) | copy-start | bytes 4325380

commit v2 on v1

v2 whole, which is shorter than its diff:
```python
import dataclasses
import functools

import jax
import jax.numpy as jnp
from jax import lax
from jax.experimental import pallas as pl
from jax.experimental.pallas import tpu as pltpu
from jax.sharding import PartitionSpec as P

MESH = pl.DeviceIdType.MESH
F32 = jnp.float32
BF16 = jnp.bfloat16
LANES = 128
CW = 3 * LANES


@dataclasses.dataclass(frozen=True)
class Sizes:
    n_dp: int
    n_x: int
    tok: int
    top: int
    cap: int
    width: int
    ff: int

    @property
    def rows(self):
        return self.n_dp * self.n_x * self.cap

    @property
    def mix(self):
        return self.width // CW

    @property
    def fwd(self):
        return 2 * self.mix + 1

    @property
    def ret(self):
        return self.mix + 1


def dot_nn(a, b):
    return lax.dot_general(a, b, (((1,), (0,)), ((), ())), preferred_element_type=F32)


def dot_nt(a, b):
    return lax.dot_general(a, b, (((1,), (1,)), ((), ())), preferred_element_type=F32)


def onehot(cond):
    return jnp.where(cond, 1.0, 0.0).astype(BF16)


def log2(n):
    assert n & (n - 1) == 0
    return n.bit_length() - 1


def kernel(
    z, routes_ref, gates_ref, tok_ref, dy_ref, wg_hbm, wu_hbm, wd_hbm,
    out_tok, out_gate, down_hbm,
    out_down, place_ref, gate_slots_ref, xc, sel, rx, sd, g, wg, wu, wd0, wd, pg, pu, hf, ht, bh, gt, gg, gu, gp, mats, pt,
    os_, ora, orb, am, ap, arp, arm, rd, rb, sx, hb,
    w_sem, d_sem, xs, xr, ds_, dr, ys, yra, yrb, yrc, yrd,
    os_s, ora_r, orb_r, a_s, arp_r, arm_r, rd_s, rb_r, sx_s, hb_r,
):
    dp = lax.axis_index("dp")
    x = lax.axis_index("expert")
    y = lax.axis_index("tensor")
    rows, cap, n_dp, n_x, mix = z.rows, z.cap, z.n_dp, z.n_x, z.mix
    half = rows // 2
    xb, db = n_dp * cap, n_x * cap
    up, down, far = lax.rem(y + 1, 4), lax.rem(y + 3, 4), lax.rem(y + 2, 4)
    dev_up, dev_down = (dp, x, up), (dp, x, down)

    def wcopy(i):
        if i == 0:
            return pltpu.make_async_copy(wg_hbm, wg, w_sem.at[0])
        if i == 1:
            return pltpu.make_async_copy(wu_hbm, wu, w_sem.at[1])
        if i == 2:
            return pltpu.make_async_copy(wd_hbm.at[:, pl.ds(0, LANES)], wd0, w_sem.at[2])
        j = i - 3
        return pltpu.make_async_copy(
            wd_hbm.at[:, pl.ds(LANES + j * CW, CW)], wd.at[j], w_sem.at[i]
        )

    def down_copy(j):
        if isinstance(j, int) and j == mix:
            cols = pl.ds(0, LANES)
        else:
            cols = pl.ds(pl.multiple_of(LANES + j * CW, LANES), CW)
        return pltpu.make_async_copy(out_down.at[:, cols], down_hbm.at[:, cols], d_sem.at[j])

    for i in range(3 + mix):
        wcopy(i).start()

    barrier = pltpu.get_barrier_semaphore()

    def greet_dp(j, c):
        pl.semaphore_signal(
            barrier, inc=1, device_id=(lax.rem(dp + j, n_dp), x, y), device_id_type=MESH
        )
        return c

    def greet_x(j, c):
        pl.semaphore_signal(
            barrier, inc=1, device_id=(dp, lax.rem(x + j, n_x), y), device_id_type=MESH
        )
        return c

    lax.fori_loop(1, n_dp, greet_dp, 0)
    lax.fori_loop(1, n_x, greet_x, 0)
    pl.semaphore_signal(barrier, inc=1, device_id=dev_up, device_id_type=MESH)
    pl.semaphore_signal(barrier, inc=1, device_id=dev_down, device_id_type=MESH)

    slot = lax.broadcasted_iota(jnp.int32, (rows, z.tok), 0)
    s_x = slot >> log2(xb)
    s_dp = (slot & (xb - 1)) >> log2(cap)
    s_rank = slot & (cap - 1)
    s_e = s_dp * n_x + s_x
    named = jnp.zeros((rows, z.tok), F32)
    gate = jnp.zeros((rows, z.tok), F32)
    for k in range(z.top):
        hit = routes_ref[k : k + 1, :] == s_e
        named = jnp.where(hit, 1.0, named)
        gate = jnp.where(hit, gates_ref[k : k + 1, :].astype(F32), gate)
    t_row = lax.broadcasted_iota(jnp.int32, (z.tok, z.tok), 0)
    t_col = lax.broadcasted_iota(jnp.int32, (z.tok, z.tok), 1)
    rank = dot_nn(named.astype(BF16), onehot(t_row < t_col))
    picked = jnp.where(rank == s_rank.astype(F32), named, 0.0)
    place_ref[...] = picked.astype(BF16)
    gate_slots_ref[...] = dot_nn(
        (picked * gate).astype(BF16), jnp.ones((z.tok, LANES), BF16)
    ).astype(BF16)
    for q in range(mix):
        xc[q] = tok_ref[:, q * CW : (q + 1) * CW]
        xc[mix + 1 + q] = dy_ref[:, LANES + q * CW : LANES + (q + 1) * CW]
    xc[mix, :, 0:LANES] = tok_ref[:, mix * CW :]
    xc[mix, :, LANES : 2 * LANES] = jnp.zeros((z.tok, LANES), BF16)
    xc[mix, :, 2 * LANES :] = dy_ref[:, 0:LANES]

    def choose(q):
        sel[q] = dot_nn(place_ref[...], xc[q]).astype(BF16)

    for q in range(min(2, z.fwd)):
        choose(q)

    pl.semaphore_wait(barrier, n_dp - 1 + n_x - 1 + 2)

    def remote(src, dst, send, recv, dev):
        return pltpu.make_async_remote_copy(
            src_ref=src, dst_ref=dst, send_sem=send, recv_sem=recv,
            device_id=dev, device_id_type=MESH,
        )

    def got(region, sem):
        remote(region, region, sem, sem, dev_up).wait_recv()

    def left(region, sem):
        remote(region, region, sem, sem, dev_up).wait_send()

    def f0(q):
        @pl.when(q >= 2)
        def _():
            choose(q)

        @pl.when(q == mix)
        def _():
            sel[q, :, LANES : 2 * LANES] = gate_slots_ref[...]

        rx[q, pl.ds(pl.multiple_of(x * xb, 16), xb)] = sel[q, pl.ds(pl.multiple_of(x * xb, 16), xb)]

        def send(j, c):
            to = lax.rem(x + j, n_x)
            remote(
                sel.at[q, pl.ds(pl.multiple_of(to * xb, 16), xb)],
                rx.at[q, pl.ds(pl.multiple_of(x * xb, 16), xb)],
                xs.at[q], xr.at[q], (dp, to, y),
            ).start()
            return c

        lax.fori_loop(1, n_x, send, 0)

    def f1(q):
        got(rx.at[q, pl.ds(0, rows - xb)], xr.at[q])
        sd[q] = dot_nn(mats[0], rx[q]).astype(BF16)
        mine = pl.ds(pl.multiple_of(dp * db, 16), db)

        def send(j, c):
            to = lax.rem(dp + j, n_dp)
            remote(
                sd.at[q, pl.ds(pl.multiple_of(to * db, 16), db)],
                g.at[q, y, mine],
                ds_.at[q], dr.at[q], (to, x, y),
            ).start()
            return c

        lax.fori_loop(1, n_dp, send, 0)
        g[q, y, mine] = sd[q, mine]

    def f2(q):
        got(g.at[q, y, pl.ds(0, rows - db)], dr.at[q])
        remote(g.at[q, y], g.at[q, y], ys.at[q], yra.at[q], dev_up).start()
        remote(g.at[q, y], g.at[q, y], ys.at[q], yrb.at[q], dev_down).start()

    def f3(q):
        got(g.at[q, down], yra.at[q])
        first = g.at[q, down, pl.ds(0, half)]
        remote(first, first, ys.at[q], yrc.at[q], dev_up).start()
        got(g.at[q, up], yrb.at[q])
        second = g.at[q, up, pl.ds(half, half)]
        remote(second, second, ys.at[q], yrd.at[q], dev_down).start()

    def f4(q):
        got(g.at[q, far, pl.ds(0, half)], yrc.at[q])
        got(g.at[q, far, pl.ds(half, half)], yrd.at[q])

        @pl.when(q == 0)
        def _():
            def one(o, c):
                pg[o] = dot_nt(g[q, o], wg[:, 0:CW])
                pu[o] = dot_nt(g[q, o], wu[:, 0:CW])
                return c

            lax.fori_loop(0, 4, one, 0)

        @pl.when(jnp.logical_and(q > 0, q < mix))
        def _():
            part = pl.ds(pl.multiple_of(q * CW, LANES), CW)

            def one(o, c):
                pg[o] += dot_nt(g[q, o], wg[:, part])
                pu[o] += dot_nt(g[q, o], wu[:, part])
                return c

            lax.fori_loop(0, 4, one, 0)

        @pl.when(q == mix)
        def _():
            def one(o, down_acc):
                xe = g[q, o, :, 0:LANES]
                tail = pl.ds(mix * CW, LANES)
                pre_gate = pg[o] + dot_nt(xe, wg[:, tail])
                pre_up = pu[o] + dot_nt(xe, wu[:, tail])
                sig = 1.0 / (1.0 + jnp.exp(-pre_gate))
                act = pre_gate * sig
                hidden = act * pre_up
                pg[o] = act
                pu[o] = pre_up * sig * (1.0 + pre_gate * (1.0 - sig))
                hf[o] = hidden
                r = lax.broadcasted_iota(jnp.int32, (z.ff, z.ff), 0)
                c = lax.broadcasted_iota(jnp.int32, (z.ff, z.ff), 1)
                ht[o] = dot_nt(onehot(r == c), hidden.astype(BF16)).astype(BF16)
                gt[o] = g[q, o, :, LANES : 2 * LANES].astype(F32)
                dye = g[q, o, :, 2 * LANES : 3 * LANES]
                bh[o] = dot_nt(dye, wd0[...])
                weighted = (gt[o] * dye.astype(F32)).astype(BF16)
                return down_acc + dot_nn(ht[o], weighted)

            out_down[:, 0:LANES] = lax.fori_loop(0, 4, one, jnp.zeros((z.ff, LANES), F32))
            down_copy(mix).start()

        @pl.when(q > mix)
        def _():
            j = q - mix - 1

            def one(o, c):
                bh[o] += dot_nt(g[q, o], wd[j])
                return c

            lax.fori_loop(0, 4, one, 0)

        pl.when(jnp.logical_and(q > mix, q < z.fwd - 1))(functools.partial(grad_down, q))

    def grad_down(q):
        j = q - mix - 1
        cols = pl.ds(pl.multiple_of(LANES + j * CW, LANES), CW)

        def weighted(o):
            scale = jnp.concatenate([gt[o]] * 3, axis=1)
            return (scale * g[q, o].astype(F32)).astype(BF16)

        total = dot_nn(ht[0], weighted(0))
        for o in range(1, 4):
            total += dot_nn(ht[o], weighted(o))
        out_down[:, cols] = total
        down_copy(j).start()

    def at(t, n, do):
        pl.when(jnp.logical_and(t >= 0, t < n))(functools.partial(do, t))

    for q in range(min(3, z.fwd)):
        f0(jnp.int32(q))
    pt[...] = dot_nt(onehot(t_row == t_col), place_ref[...]).astype(BF16)
    i_row = lax.broadcasted_iota(jnp.int32, (rows, rows), 0)
    i_col = lax.broadcasted_iota(jnp.int32, (rows, rows), 1)

    def reordered(i):
        return (
            ((i & (db - 1)) >> log2(cap)) * xb + (i >> log2(db)) * cap + (i & (cap - 1))
        )

    mats[0] = onehot(i_col == reordered(i_row))
    mats[1] = onehot(i_row == reordered(i_col))


    for i in range(3 + mix):
        wcopy(i).wait()

    def tick_out(t, c):
        at(t - 4, z.fwd, f3)
        at(t - 2, z.fwd, f2)
        at(t, z.fwd, f1)
        at(t + 3, z.fwd, f0)
        at(t - 5, z.fwd, f4)
        return c

    lax.fori_loop(0, z.fwd + 5, tick_out, 0)

    def middle(o):
        back_h = bh[o]
        scaled = gt[o][:, 0:1] * back_h
        gg[o] = (scaled * pu[o]).astype(BF16)
        gu[o] = (scaled * pg[o]).astype(BF16)
        gp[o] = jnp.broadcast_to(
            jnp.sum(hf[o] * back_h, axis=1, keepdims=True), (rows, LANES)
        )

    def partial_rows(o, r, w):
        if w == CW:
            part = pl.ds(pl.multiple_of(r * CW, LANES), CW)
            return dot_nn(gg[o], wg[:, part]) + dot_nn(gu[o], wu[:, part])
        tail = pl.ds(mix * CW, LANES)
        total = dot_nn(gg[o], wg[:, tail]) + dot_nn(gu[o], wu[:, tail])
        return jnp.concatenate([total, gp[o]], axis=1)

    lo, hi = pl.ds(0, half), pl.ds(half, half)

    def r0(r, w):
        cs = pl.ds(0, w)
        os_[r, :, cs] = partial_rows(far, r, w).astype(BF16)
        remote(os_.at[r, lo, cs], ora.at[r, :, cs], os_s.at[r], ora_r.at[r], dev_down).start()
        remote(os_.at[r, hi, cs], orb.at[r, :, cs], os_s.at[r], orb_r.at[r], dev_up).start()

    def r1(r, w):
        cs = pl.ds(0, w)
        mine = partial_rows(down, r, w)
        got(ora.at[r, :, cs], ora_r.at[r])
        am[r, lo, cs] = (mine[0:half] + ora[r, :, cs].astype(F32)).astype(BF16)
        am[r, hi, cs] = mine[half:].astype(BF16)
        remote(am.at[r, :, cs], arp.at[r, :, cs], a_s.at[r], arp_r.at[r], dev_down).start()
        mine = partial_rows(up, r, w)
        got(orb.at[r, :, cs], orb_r.at[r])
        ap[r, lo, cs] = mine[0:half].astype(BF16)
        ap[r, hi, cs] = (mine[half:] + orb[r, :, cs].astype(F32)).astype(BF16)
        remote(ap.at[r, :, cs], arm.at[r, :, cs], a_s.at[r], arm_r.at[r], dev_up).start()

    def r2(r, w):
        cs = pl.ds(0, w)
        mine = partial_rows(y, r, w)
        got(arp.at[r, :, cs], arp_r.at[r])
        got(arm.at[r, :, cs], arm_r.at[r])
        rd[r, :, cs] = (
            mine + arp[r, :, cs].astype(F32) + arm[r, :, cs].astype(F32)
        ).astype(BF16)
        own = pl.ds(pl.multiple_of(dp * db, 16), db)

        def send(j, c):
            to = lax.rem(dp + j, n_dp)
            remote(
                rd.at[r, pl.ds(pl.multiple_of(to * db, 16), db), cs], rb.at[r, own, cs],
                rd_s.at[r], rb_r.at[r], (to, x, y),
            ).start()
            return c

        lax.fori_loop(1, n_dp, send, 0)
        rb[r, own, cs] = rd[r, own, cs]

    def r3(r, w):
        cs = pl.ds(0, w)
        got(rb.at[r, pl.ds(0, rows - db), cs], rb_r.at[r])
        sx[r, :, cs] = dot_nn(mats[1], rb[r, :, cs]).astype(BF16)
        own = pl.ds(pl.multiple_of(x * xb, 16), xb)

        def send(j, c):
            to = lax.rem(x + j, n_x)
            remote(
                sx.at[r, pl.ds(pl.multiple_of(to * xb, 16), xb), cs], hb.at[r, own, cs],
                sx_s.at[r], hb_r.at[r], (dp, to, y),
            ).start()
            return c

        lax.fori_loop(1, n_x, send, 0)
        hb[r, own, cs] = sx[r, own, cs]

    def r4(r, w):
        got(hb.at[r, pl.ds(0, rows - xb), pl.ds(0, w)], hb_r.at[r])
        if w == CW:
            cols = pl.ds(pl.multiple_of(r * CW, LANES), CW)
            out_tok[:, cols] = dot_nn(pt[...], hb[r]).astype(BF16)
            return
        out_tok[:, mix * CW :] = dot_nn(pt[...], hb[r, :, 0:LANES]).astype(BF16)
        row = lax.broadcasted_iota(jnp.int32, (rows, LANES), 0)
        lane = lax.broadcasted_iota(jnp.int32, (rows, LANES), 1)
        e = ((row & (xb - 1)) >> log2(cap)) * n_x + (row >> log2(xb))
        vals = jnp.where(e == lane, hb[r, :, LANES : 2 * LANES].astype(F32), 0.0)
        by_expert = dot_nn(pt[...], vals.astype(BF16))
        e_row = lax.broadcasted_iota(jnp.int32, (LANES, LANES), 0)
        e_col = lax.broadcasted_iota(jnp.int32, (LANES, LANES), 1)
        by_expert = dot_nt(onehot(e_row == e_col), by_expert.astype(BF16))
        e_tok = lax.broadcasted_iota(jnp.int32, (LANES, z.tok), 0)
        for k in range(z.top):
            hit = routes_ref[k : k + 1, :] == e_tok
            out_gate[k : k + 1, :] = jnp.sum(
                jnp.where(hit, by_expert, 0.0), axis=0, keepdims=True
            ).astype(BF16)

    def back(t, do):
        pl.when(jnp.logical_and(t >= 0, t < mix))(functools.partial(do, t, CW))
        pl.when(t == mix)(functools.partial(do, t, 2 * LANES))

    def tick_back(t, c):
        back(t - 2, r1)
        back(t, r0)
        back(t - 4, r2)
        back(t - 6, r3)
        back(t - 8, r4)
        return c

    middle(far)
    r0(0, CW)
    for o in (down, up, y):
        middle(o)
    grad_down(z.fwd - 1)
    lax.fori_loop(1, z.ret + 8, tick_back, 0)

    def drain_out(q, c):
        left(sel.at[q, pl.ds(0, rows - xb)], xs.at[q])
        left(sd.at[q, pl.ds(0, rows - db)], ds_.at[q])
        left(g.at[q, pl.ds(0, 3)], ys.at[q])
        return c

    def drain_back(r, w):
        cs = pl.ds(0, w)
        left(os_.at[r, :, cs], os_s.at[r])
        left(g.at[r, pl.ds(0, 2), :, cs], a_s.at[r])
        left(rd.at[r, pl.ds(0, rows - db), cs], rd_s.at[r])
        left(sx.at[r, pl.ds(0, rows - xb), cs], sx_s.at[r])

    lax.fori_loop(0, z.fwd, drain_out, 0)
    for j in range(mix + 1):
        down_copy(j).wait()
    for r in range(mix):
        drain_back(r, CW)
    drain_back(mix, 2 * LANES)


def hand_over(tok_in, gate_in, down_in, tok_out, gate_out, down_out, tok, gate, down, sem):
    parts = [(tok_in, tok, tok_out), (gate_in, gate, gate_out)]
    step = down.shape[0] // 4
    for i in range(4):
        part = pl.ds(i * step, step)
        parts.append((down_in.at[part], down.at[part], down_out.at[part]))
    reads = [
        pltpu.make_async_copy(a, b, sem.at[0, i]) for i, (a, b, _) in enumerate(parts)
    ]
    writes = [
        pltpu.make_async_copy(b, c, sem.at[1, i]) for i, (_, b, c) in enumerate(parts)
    ]
    for read in reads:
        read.start()
    for read, write in zip(reads, writes):
        read.wait()
        write.start()
    for write in writes:
        write.wait()


def body(cap, tokens, out_grad, routes, gates, w_gate, w_up, w_down):
    z = Sizes(
        n_dp=lax.axis_size("dp"), n_x=lax.axis_size("expert"), tok=tokens.shape[0],
        top=routes.shape[1], cap=cap, width=tokens.shape[1], ff=w_gate.shape[2],
    )
    assert lax.axis_size("tensor") == 4 and z.width % CW == LANES
    rows, half, fwd, ret, mix = z.rows, z.rows // 2, z.fwd, z.ret, z.mix
    vm = pltpu.VMEM
    sem = pltpu.SemaphoreType.DMA
    scratch = [
        vm((z.ff, z.width), F32),
        vm((rows, z.tok), BF16),
        vm((rows, LANES), BF16),
        vm((fwd, z.tok, CW), BF16),
        vm((fwd, rows, CW), BF16),
        vm((fwd, rows, CW), BF16),
        vm((fwd, rows, CW), BF16),
        vm((fwd, 4, rows, CW), BF16),
        vm((z.ff, z.width), BF16),
        vm((z.ff, z.width), BF16),
        vm((z.ff, LANES), BF16),
        vm((mix, z.ff, CW), BF16),
        vm((4, rows, z.ff), F32),
        vm((4, rows, z.ff), F32),
        vm((4, rows, z.ff), F32),
        vm((4, z.ff, rows), BF16),
        vm((4, rows, z.ff), F32),
        vm((4, rows, LANES), F32),
        vm((4, rows, z.ff), BF16),
        vm((4, rows, z.ff), BF16),
        vm((4, rows, LANES), F32),
        vm((2, rows, rows), BF16),
        vm((z.tok, rows), BF16),
        vm((ret, rows, CW), BF16),
        vm((ret, half, CW), BF16),
        vm((ret, half, CW), BF16),
        vm((ret, rows, CW), BF16),
        vm((ret, rows, CW), BF16),
        vm((ret, rows, CW), BF16),
        vm((ret, rows, CW), BF16),
        vm((ret, rows, CW), BF16),
        vm((ret, rows, CW), BF16),
        vm((ret, rows, CW), BF16),
        vm((ret, rows, CW), BF16),
        sem((3 + mix,)),
        sem((mix + 1,)),
    ] + [sem((fwd,))] * 9 + [sem((ret,))] * 10
    vmem = pl.BlockSpec(memory_space=pltpu.VMEM)
    hbm = pl.BlockSpec(memory_space=pl.ANY)
    grad_tokens, grad_gate, grad_down = pl.pallas_call(
        functools.partial(kernel, z),
        out_shape=(
            jax.ShapeDtypeStruct((z.tok, z.width), BF16),
            jax.ShapeDtypeStruct((z.top, z.tok), BF16),
            jax.ShapeDtypeStruct((z.ff, z.width), F32),
        ),
        in_specs=[vmem] * 4 + [hbm] * 3,
        out_specs=(vmem, vmem, hbm),
        scratch_shapes=scratch,
        compiler_params=pltpu.CompilerParams(
            collective_id=0, has_side_effects=True, vmem_limit_bytes=60 * 1024 * 1024
        ),
    )(routes.T, gates.T, tokens, out_grad, w_gate[0].T, w_up[0].T, w_down[0])
    results = (grad_tokens, grad_gate, grad_down)
    grad_tokens, grad_gate, grad_down = pl.pallas_call(
        hand_over,
        out_shape=tuple(jax.ShapeDtypeStruct(r.shape, r.dtype) for r in results),
        in_specs=[hbm] * 3,
        out_specs=(hbm,) * 3,
        scratch_shapes=[vm(r.shape, r.dtype) for r in results] + [sem((2, 6))],
    )(*results)
    return grad_tokens, grad_gate.T, grad_down[None]


def solution(mesh, cap=4):
    tokens = P(("dp", "expert", "tensor"), None)
    return jax.shard_map(
        functools.partial(body, cap),
        mesh=mesh,
        in_specs=(
            tokens, tokens, tokens, tokens,
            P(("dp", "expert"), None, "tensor"),
            P(("dp", "expert"), None, "tensor"),
            P(("dp", "expert"), "tensor", None),
        ),
        out_specs=(tokens, tokens, P(("dp", "expert"), "tensor", None)),
        check_vma=False,
    )
```

time: 188 us -> 157 us (0.84)
  Pallas kernels: 174 us -> 156 us
  local copies, waits for them, and re-layouts: 13.6 us -> 0 us
    pallas_call x1, Pallas kernels: 174 us -> 153 us  [body(): pl.pallas_call(functools.partial(kernel, z), out_shape=(jax.ShapeDtypeStr...]
    unnamed x9 -> x0, local copies, waits for them, and re-layouts: 13.6 us -> none
    pallas_call x0 -> x1, Pallas kernels: none -> 2.87 us  [body(): pl.pallas_call(hand_over, out_shape=tuple((jax.ShapeDtypeStruct(r.shape,...]
where the time goes in v2:
time: 157 us
  Pallas kernels  156 us (99%)
    pallas_call x1, Pallas kernels, body(): pl.pallas_call(functools.partial(kernel, z), out_shape=(jax.ShapeDtypeStr...  153 us

profile of v2, /device:TPU:1, one launch (start us, length us, event | category | flops | bytes accessed | tf_op | source)
XLA Modules:
  0.0 156.5 jit_solution(4021989198516831210)
XLA Ops:
  0.6 153.0 %shard_map.94 = (bf16[32,2048]{1,0:T(8,128)(2,1)}, bf16[6,32]{1,0:T(8,128)(2,1)}, f32[352,2048]{1,0:T(8,128)}) custom-call(s32[6,32]{1,0:T(8,128)} %bitcast.14, bf16[6,32]{1,0:T(8,128)(2,1)} %bitcast.15, bf16[32,2048]{1,0:T(8,128)(2,1)} %tok_ref.1, bf16[32,2048]{1,0:T(8,128)(2,1)} %dy_ref.1, bf16[352,2048]{1,0:T(8,128)(2,1)} %bitcast.11, ...), custom_call_target="tpu_custom_call" | custom-call | tf_op jit(solution)/shard_map/pallas_call | solution.py:532
  153.7 2.9 %shard_map.95 = (bf16[32,2048]{1,0:T(8,128)(2,1)}, bf16[6,32]{1,0:T(8,128)(2,1)}, f32[352,2048]{1,0:T(8,128)}) custom-call(bf16[32,2048]{1,0:T(8,128)(2,1)} %get-tuple-element.9.tok_in, bf16[6,32]{1,0:T(8,128)(2,1)} %get-tuple-element.10.gate_in, f32[352,2048]{1,0:T(8,128)} %get-tuple-element.11.down_in), custom_call_target="tpu_custom_call" | custom-call | tf_op jit(solution)/shard_map/pallas_call | solution.py:547

commit v3 on v2

--- a/solution.py
+++ b/solution.py
@@ -12,7 +12,8 @@
 F32 = jnp.float32
 BF16 = jnp.bfloat16
 LANES = 128
-CW = 3 * LANES
+CW = 2 * LANES
+AHEAD = 4
 
 
 @dataclasses.dataclass(frozen=True)
@@ -62,7 +63,7 @@
 def kernel(
     z, routes_ref, gates_ref, tok_ref, dy_ref, wg_hbm, wu_hbm, wd_hbm,
     out_tok, out_gate, down_hbm,
-    out_down, place_ref, gate_slots_ref, xc, sel, rx, sd, g, wg, wu, wd0, wd, pg, pu, hf, ht, bh, gt, gg, gu, gp, mats, pt,
+    out_down, place_ref, xc, sel, rx, sd, g, wg, wu, wd, pg, pu, hf, ht, bh, gt, gg, gu, gp, mats, pt,
     os_, ora, orb, am, ap, arp, arm, rd, rb, sx, hb,
     w_sem, d_sem, xs, xr, ds_, dr, ys, yra, yrb, yrc, yrd,
     os_s, ora_r, orb_r, a_s, arp_r, arm_r, rd_s, rb_r, sx_s, hb_r,
@@ -81,21 +82,16 @@
             return pltpu.make_async_copy(wg_hbm, wg, w_sem.at[0])
         if i == 1:
             return pltpu.make_async_copy(wu_hbm, wu, w_sem.at[1])
-        if i == 2:
-            return pltpu.make_async_copy(wd_hbm.at[:, pl.ds(0, LANES)], wd0, w_sem.at[2])
-        j = i - 3
+        j = i - 2
         return pltpu.make_async_copy(
-            wd_hbm.at[:, pl.ds(LANES + j * CW, CW)], wd.at[j], w_sem.at[i]
+            wd_hbm.at[:, pl.ds(j * CW, CW)], wd.at[j], w_sem.at[i]
         )
 
     def down_copy(j):
-        if isinstance(j, int) and j == mix:
-            cols = pl.ds(0, LANES)
-        else:
-            cols = pl.ds(pl.multiple_of(LANES + j * CW, LANES), CW)
+        cols = pl.ds(pl.multiple_of(j * CW, CW), CW)
         return pltpu.make_async_copy(out_down.at[:, cols], down_hbm.at[:, cols], d_sem.at[j])
 
-    for i in range(3 + mix):
+    for i in range(2 + mix):
         wcopy(i).start()
 
     barrier = pltpu.get_barrier_semaphore()
@@ -133,21 +129,17 @@
     rank = dot_nn(named.astype(BF16), onehot(t_row < t_col))
     picked = jnp.where(rank == s_rank.astype(F32), named, 0.0)
     place_ref[...] = picked.astype(BF16)
-    gate_slots_ref[...] = dot_nn(
+    sel[0, :, 0:LANES] = dot_nn(
         (picked * gate).astype(BF16), jnp.ones((z.tok, LANES), BF16)
     ).astype(BF16)
     for q in range(mix):
-        xc[q] = tok_ref[:, q * CW : (q + 1) * CW]
-        xc[mix + 1 + q] = dy_ref[:, LANES + q * CW : LANES + (q + 1) * CW]
-    xc[mix, :, 0:LANES] = tok_ref[:, mix * CW :]
-    xc[mix, :, LANES : 2 * LANES] = jnp.zeros((z.tok, LANES), BF16)
-    xc[mix, :, 2 * LANES :] = dy_ref[:, 0:LANES]
+        xc[1 + q] = tok_ref[:, q * CW : (q + 1) * CW]
+        xc[1 + mix + q] = dy_ref[:, q * CW : (q + 1) * CW]
 
     def choose(q):
         sel[q] = dot_nn(place_ref[...], xc[q]).astype(BF16)
 
-    for q in range(min(2, z.fwd)):
-        choose(q)
+    choose(1)
 
     pl.semaphore_wait(barrier, n_dp - 1 + n_x - 1 + 2)
 
@@ -163,63 +155,66 @@
     def left(region, sem):
         remote(region, region, sem, sem, dev_up).wait_send()
 
-    def f0(q):
-        @pl.when(q >= 2)
-        def _():
-            choose(q)
-
-        @pl.when(q == mix)
-        def _():
-            sel[q, :, LANES : 2 * LANES] = gate_slots_ref[...]
-
-        rx[q, pl.ds(pl.multiple_of(x * xb, 16), xb)] = sel[q, pl.ds(pl.multiple_of(x * xb, 16), xb)]
+    def f0(q, w):
+        cs = pl.ds(0, w)
+        if w == CW:
+            pl.when(q > 1)(functools.partial(choose, q))
+        mine = pl.ds(pl.multiple_of(x * xb, 16), xb)
+        rx[q, mine, cs] = sel[q, mine, cs]
 
         def send(j, c):
             to = lax.rem(x + j, n_x)
             remote(
-                sel.at[q, pl.ds(pl.multiple_of(to * xb, 16), xb)],
-                rx.at[q, pl.ds(pl.multiple_of(x * xb, 16), xb)],
+                sel.at[q, pl.ds(pl.multiple_of(to * xb, 16), xb), cs], rx.at[q, mine, cs],
                 xs.at[q], xr.at[q], (dp, to, y),
             ).start()
             return c
 
         lax.fori_loop(1, n_x, send, 0)
 
-    def f1(q):
-        got(rx.at[q, pl.ds(0, rows - xb)], xr.at[q])
-        sd[q] = dot_nn(mats[0], rx[q]).astype(BF16)
+    def f1(q, w):
+        cs = pl.ds(0, w)
+        got(rx.at[q, pl.ds(0, rows - xb), cs], xr.at[q])
+        sd[q, :, cs] = dot_nn(mats[0], rx[q, :, cs]).astype(BF16)
         mine = pl.ds(pl.multiple_of(dp * db, 16), db)
 
         def send(j, c):
             to = lax.rem(dp + j, n_dp)
             remote(
-                sd.at[q, pl.ds(pl.multiple_of(to * db, 16), db)],
-                g.at[q, y, mine],
+                sd.at[q, pl.ds(pl.multiple_of(to * db, 16), db), cs], g.at[q, y, mine, cs],
                 ds_.at[q], dr.at[q], (to, x, y),
             ).start()
             return c
 
         lax.fori_loop(1, n_dp, send, 0)
-        g[q, y, mine] = sd[q, mine]
-
-    def f2(q):
-        got(g.at[q, y, pl.ds(0, rows - db)], dr.at[q])
-        remote(g.at[q, y], g.at[q, y], ys.at[q], yra.at[q], dev_up).start()
-        remote(g.at[q, y], g.at[q, y], ys.at[q], yrb.at[q], dev_down).start()
-
-    def f3(q):
-        got(g.at[q, down], yra.at[q])
-        first = g.at[q, down, pl.ds(0, half)]
+        g[q, y, mine, cs] = sd[q, mine, cs]
+
+    def f2(q, w):
+        cs = pl.ds(0, w)
+        got(g.at[q, y, pl.ds(0, rows - db), cs], dr.at[q])
+        whole = g.at[q, y, :, cs]
+        remote(whole, whole, ys.at[q], yra.at[q], dev_up).start()
+        remote(whole, whole, ys.at[q], yrb.at[q], dev_down).start()
+
+    def f3(q, w):
+        cs = pl.ds(0, w)
+        got(g.at[q, down, :, cs], yra.at[q])
+        first = g.at[q, down, pl.ds(0, half), cs]
         remote(first, first, ys.at[q], yrc.at[q], dev_up).start()
-        got(g.at[q, up], yrb.at[q])
-        second = g.at[q, up, pl.ds(half, half)]
+        got(g.at[q, up, :, cs], yrb.at[q])
+        second = g.at[q, up, pl.ds(half, half), cs]
         remote(second, second, ys.at[q], yrd.at[q], dev_down).start()
 
-    def f4(q):
-        got(g.at[q, far, pl.ds(0, half)], yrc.at[q])
-        got(g.at[q, far, pl.ds(half, half)], yrd.at[q])
-
-        @pl.when(q == 0)
+    def f4(q, w):
+        cs = pl.ds(0, w)
+        got(g.at[q, far, pl.ds(0, half), cs], yrc.at[q])
+        got(g.at[q, far, pl.ds(half, half), cs], yrd.at[q])
+        if w != CW:
+            for o in range(4):
+                gt[o] = g[q, o, :, cs].astype(F32)
+            return
+
+        @pl.when(q == 1)
         def _():
             def one(o, c):
                 pg[o] = dot_nt(g[q, o], wg[:, 0:CW])
@@ -228,9 +223,9 @@
 
             lax.fori_loop(0, 4, one, 0)
 
-        @pl.when(jnp.logical_and(q > 0, q < mix))
+        @pl.when(jnp.logical_and(q > 1, q <= mix))
         def _():
-            part = pl.ds(pl.multiple_of(q * CW, LANES), CW)
+            part = pl.ds(pl.multiple_of((q - 1) * CW, CW), CW)
 
             def one(o, c):
                 pg[o] += dot_nt(g[q, o], wg[:, part])
@@ -241,35 +236,34 @@
 
         @pl.when(q == mix)
         def _():
-            def one(o, down_acc):
-                xe = g[q, o, :, 0:LANES]
-                tail = pl.ds(mix * CW, LANES)
-                pre_gate = pg[o] + dot_nt(xe, wg[:, tail])
-                pre_up = pu[o] + dot_nt(xe, wu[:, tail])
+            def one(o, c):
+                pre_gate = pg[o]
+                pre_up = pu[o]
                 sig = 1.0 / (1.0 + jnp.exp(-pre_gate))
                 act = pre_gate * sig
                 hidden = act * pre_up
                 pg[o] = act
                 pu[o] = pre_up * sig * (1.0 + pre_gate * (1.0 - sig))
                 hf[o] = hidden
-                r = lax.broadcasted_iota(jnp.int32, (z.ff, z.ff), 0)
-                c = lax.broadcasted_iota(jnp.int32, (z.ff, z.ff), 1)
-                ht[o] = dot_nt(onehot(r == c), hidden.astype(BF16)).astype(BF16)
-                gt[o] = g[q, o, :, LANES : 2 * LANES].astype(F32)
-                dye = g[q, o, :, 2 * LANES : 3 * LANES]
-                bh[o] = dot_nt(dye, wd0[...])
-                weighted = (gt[o] * dye.astype(F32)).astype(BF16)
-                return down_acc + dot_nn(ht[o], weighted)
-
-            out_down[:, 0:LANES] = lax.fori_loop(0, 4, one, jnp.zeros((z.ff, LANES), F32))
-            down_copy(mix).start()
-
-        @pl.when(q > mix)
+                f_row = lax.broadcasted_iota(jnp.int32, (z.ff, z.ff), 0)
+                f_col = lax.broadcasted_iota(jnp.int32, (z.ff, z.ff), 1)
+                ht[o] = dot_nt(onehot(f_row == f_col), hidden.astype(BF16)).astype(BF16)
+                return c
+
+            lax.fori_loop(0, 4, one, 0)
+
+        @pl.when(q == mix + 1)
         def _():
-            j = q - mix - 1
-
             def one(o, c):
-                bh[o] += dot_nt(g[q, o], wd[j])
+                bh[o] = dot_nt(g[q, o], wd[0])
+                return c
+
+            lax.fori_loop(0, 4, one, 0)
+
+        @pl.when(q > mix + 1)
+        def _():
+            def one(o, c):
+                bh[o] += dot_nt(g[q, o], wd[q - mix - 1])
                 return c
 
             lax.fori_loop(0, 4, one, 0)
@@ -278,10 +272,10 @@
 
     def grad_down(q):
         j = q - mix - 1
-        cols = pl.ds(pl.multiple_of(LANES + j * CW, LANES), CW)
+        cols = pl.ds(pl.multiple_of(j * CW, CW), CW)
 
         def weighted(o):
-            scale = jnp.concatenate([gt[o]] * 3, axis=1)
+            scale = jnp.concatenate([gt[o]] * 2, axis=1)
             return (scale * g[q, o].astype(F32)).astype(BF16)
 
         total = dot_nn(ht[0], weighted(0))
@@ -290,11 +284,13 @@
         out_down[:, cols] = total
         down_copy(j).start()
 
-    def at(t, n, do):
-        pl.when(jnp.logical_and(t >= 0, t < n))(functools.partial(do, t))
-
-    for q in range(min(3, z.fwd)):
-        f0(jnp.int32(q))
+    def at(t, do):
+        pl.when(t == 0)(functools.partial(do, t, LANES))
+        pl.when(jnp.logical_and(t > 0, t < z.fwd))(functools.partial(do, t, CW))
+
+    f0(0, LANES)
+    for q in range(1, AHEAD):
+        f0(jnp.int32(q), CW)
     pt[...] = dot_nt(onehot(t_row == t_col), place_ref[...]).astype(BF16)
     i_row = lax.broadcasted_iota(jnp.int32, (rows, rows), 0)
     i_col = lax.broadcasted_iota(jnp.int32, (rows, rows), 1)
@@ -308,15 +304,15 @@
     mats[1] = onehot(i_row == reordered(i_col))
 
 
-    for i in range(3 + mix):
+    for i in range(2 + mix):
         wcopy(i).wait()
 
     def tick_out(t, c):
-        at(t - 4, z.fwd, f3)
-        at(t - 2, z.fwd, f2)
-        at(t, z.fwd, f1)
-        at(t + 3, z.fwd, f0)
-        at(t - 5, z.fwd, f4)
+        at(t - 4, f3)
+        at(t - 2, f2)
+        at(t, f1)
+        pl.when(t + AHEAD < z.fwd)(functools.partial(f0, t + AHEAD, CW))
+        at(t - 5, f4)
         return c
 
     lax.fori_loop(0, z.fwd + 5, tick_out, 0)
@@ -331,12 +327,10 @@
         )
 
     def partial_rows(o, r, w):
-        if w == CW:
-            part = pl.ds(pl.multiple_of(r * CW, LANES), CW)
-            return dot_nn(gg[o], wg[:, part]) + dot_nn(gu[o], wu[:, part])
-        tail = pl.ds(mix * CW, LANES)
-        total = dot_nn(gg[o], wg[:, tail]) + dot_nn(gu[o], wu[:, tail])
-        return jnp.concatenate([total, gp[o]], axis=1)
+        if w != CW:
+            return gp[o]
+        part = pl.ds(pl.multiple_of(r * CW, CW), CW)
+        return dot_nn(gg[o], wg[:, part]) + dot_nn(gu[o], wu[:, part])
 
     lo, hi = pl.ds(0, half), pl.ds(half, half)
 
@@ -403,11 +397,10 @@
             cols = pl.ds(pl.multiple_of(r * CW, LANES), CW)
             out_tok[:, cols] = dot_nn(pt[...], hb[r]).astype(BF16)
             return
-        out_tok[:, mix * CW :] = dot_nn(pt[...], hb[r, :, 0:LANES]).astype(BF16)
         row = lax.broadcasted_iota(jnp.int32, (rows, LANES), 0)
         lane = lax.broadcasted_iota(jnp.int32, (rows, LANES), 1)
         e = ((row & (xb - 1)) >> log2(cap)) * n_x + (row >> log2(xb))
-        vals = jnp.where(e == lane, hb[r, :, LANES : 2 * LANES].astype(F32), 0.0)
+        vals = jnp.where(e == lane, hb[r, :, 0:LANES].astype(F32), 0.0)
         by_expert = dot_nn(pt[...], vals.astype(BF16))
         e_row = lax.broadcasted_iota(jnp.int32, (LANES, LANES), 0)
         e_col = lax.broadcasted_iota(jnp.int32, (LANES, LANES), 1)
@@ -421,7 +414,7 @@
 
     def back(t, do):
         pl.when(jnp.logical_and(t >= 0, t < mix))(functools.partial(do, t, CW))
-        pl.when(t == mix)(functools.partial(do, t, 2 * LANES))
+        pl.when(t == mix)(functools.partial(do, t, LANES))
 
     def tick_back(t, c):
         back(t - 2, r1)
@@ -438,11 +431,11 @@
     grad_down(z.fwd - 1)
     lax.fori_loop(1, z.ret + 8, tick_back, 0)
 
-    def drain_out(q, c):
-        left(sel.at[q, pl.ds(0, rows - xb)], xs.at[q])
-        left(sd.at[q, pl.ds(0, rows - db)], ds_.at[q])
-        left(g.at[q, pl.ds(0, 3)], ys.at[q])
-        return c
+    def drain_out(q, w):
+        cs = pl.ds(0, w)
+        left(sel.at[q, pl.ds(0, rows - xb), cs], xs.at[q])
+        left(sd.at[q, pl.ds(0, rows - db), cs], ds_.at[q])
+        left(g.at[q, pl.ds(0, 3), :, cs], ys.at[q])
 
     def drain_back(r, w):
         cs = pl.ds(0, w)
@@ -451,12 +444,14 @@
         left(rd.at[r, pl.ds(0, rows - db), cs], rd_s.at[r])
         left(sx.at[r, pl.ds(0, rows - xb), cs], sx_s.at[r])
 
-    lax.fori_loop(0, z.fwd, drain_out, 0)
-    for j in range(mix + 1):
+    drain_out(0, LANES)
+    for q in range(1, z.fwd):
+        drain_out(q, CW)
+    for j in range(mix):
         down_copy(j).wait()
     for r in range(mix):
         drain_back(r, CW)
-    drain_back(mix, 2 * LANES)
+    drain_back(mix, LANES)
 
 
 def hand_over(tok_in, gate_in, down_in, tok_out, gate_out, down_out, tok, gate, down, sem):
@@ -485,14 +480,13 @@
         n_dp=lax.axis_size("dp"), n_x=lax.axis_size("expert"), tok=tokens.shape[0],
         top=routes.shape[1], cap=cap, width=tokens.shape[1], ff=w_gate.shape[2],
     )
-    assert lax.axis_size("tensor") == 4 and z.width % CW == LANES
+    assert lax.axis_size("tensor") == 4 and z.width % CW == 0
     rows, half, fwd, ret, mix = z.rows, z.rows // 2, z.fwd, z.ret, z.mix
     vm = pltpu.VMEM
     sem = pltpu.SemaphoreType.DMA
     scratch = [
         vm((z.ff, z.width), F32),
         vm((rows, z.tok), BF16),
-        vm((rows, LANES), BF16),
         vm((fwd, z.tok, CW), BF16),
         vm((fwd, rows, CW), BF16),
         vm((fwd, rows, CW), BF16),
@@ -500,7 +494,6 @@
         vm((fwd, 4, rows, CW), BF16),
         vm((z.ff, z.width), BF16),
         vm((z.ff, z.width), BF16),
-        vm((z.ff, LANES), BF16),
         vm((mix, z.ff, CW), BF16),
         vm((4, rows, z.ff), F32),
         vm((4, rows, z.ff), F32),
@@ -524,8 +517,8 @@
         vm((ret, rows, CW), BF16),
         vm((ret, rows, CW), BF16),
         vm((ret, rows, CW), BF16),
-        sem((3 + mix,)),
-        sem((mix + 1,)),
+        sem((2 + mix,)),
+        sem((mix,)),
     ] + [sem((fwd,))] * 9 + [sem((ret,))] * 10
     vmem = pl.BlockSpec(memory_space=pltpu.VMEM)
     hbm = pl.BlockSpec(memory_space=pl.ANY)

time: 157 us -> 154 us (0.981)
  Pallas kernels: 156 us -> 153 us
    pallas_call x1, Pallas kernels: 153 us -> 150 us  [body(): pl.pallas_call(functools.partial(kernel, z), out_shape=(jax.ShapeDtypeStr...]
where the time goes in v3:
time: 154 us; the launch traced here: 153 us
  Pallas kernels  153 us (99%)
    pallas_call x1, Pallas kernels, body(): pl.pallas_call(functools.partial(kernel, z), out_shape=(jax.ShapeDtypeStr...  150 us

profile of v3, /device:TPU:1, one launch (start us, length us, event | category | flops | bytes accessed | tf_op | source)
XLA Modules:
  0.0 153.5 jit_solution(5633455198372903291)
XLA Ops:
  0.6 150.0 %shard_map.94 = (bf16[32,2048]{1,0:T(8,128)(2,1)}, bf16[6,32]{1,0:T(8,128)(2,1)}, f32[352,2048]{1,0:T(8,128)}) custom-call(s32[6,32]{1,0:T(8,128)} %bitcast.14, bf16[6,32]{1,0:T(8,128)(2,1)} %bitcast.15, bf16[32,2048]{1,0:T(8,128)(2,1)} %tok_ref.1, bf16[32,2048]{1,0:T(8,128)(2,1)} %dy_ref.1, bf16[352,2048]{1,0:T(8,128)(2,1)} %bitcast.11, ...), custom_call_target="tpu_custom_call" | custom-call | tf_op jit(solution)/shard_map/pallas_call | solution.py:525
  150.6 2.9 %shard_map.95 = (bf16[32,2048]{1,0:T(8,128)(2,1)}, bf16[6,32]{1,0:T(8,128)(2,1)}, f32[352,2048]{1,0:T(8,128)}) custom-call(bf16[32,2048]{1,0:T(8,128)(2,1)} %get-tuple-element.9.tok_in, bf16[6,32]{1,0:T(8,128)(2,1)} %get-tuple-element.10.gate_in, f32[352,2048]{1,0:T(8,128)} %get-tuple-element.11.down_in), custom_call_target="tpu_custom_call" | custom-call | tf_op jit(solution)/shard_map/pallas_call | solution.py:540

commit v4 on v3

--- a/solution.py
+++ b/solution.py
@@ -13,7 +13,10 @@
 BF16 = jnp.bfloat16
 LANES = 128
 CW = 2 * LANES
+LATE = 2
 AHEAD = 4
+LAGS = (3, 5, 6)
+B_START, B_STEP, B_X = 3, 2, 3
 
 
 @dataclasses.dataclass(frozen=True)
@@ -25,6 +28,7 @@
     cap: int
     width: int
     ff: int
+    late: int
 
     @property
     def rows(self):
@@ -37,6 +41,14 @@
     @property
     def fwd(self):
         return 2 * self.mix + 1
+
+    @property
+    def early(self):
+        return self.fwd - self.late
+
+    @property
+    def n_z(self):
+        return self.n_dp // 2
 
     @property
     def ret(self):
@@ -65,6 +77,8 @@
     out_tok, out_gate, down_hbm,
     out_down, place_ref, xc, sel, rx, sd, g, wg, wu, wd, pg, pu, hf, ht, bh, gt, gg, gu, gp, mats, pt,
     os_, ora, orb, am, ap, arp, arm, rd, rb, sx, hb,
+    tb, pmy, pmd, mb, pick, bsel, bx,
+    by_s, by_r, bu_r, bd_r, bz_s, bs_s, bs_r, bx_s, bx_r, pm_s, pm_r, mb_s, mb_r,
     w_sem, d_sem, xs, xr, ds_, dr, ys, yra, yrb, yrc, yrd,
     os_s, ora_r, orb_r, a_s, arp_r, arm_r, rd_s, rb_r, sx_s, hb_r,
 ):
@@ -75,7 +89,12 @@
     half = rows // 2
     xb, db = n_dp * cap, n_x * cap
     up, down, far = lax.rem(y + 1, 4), lax.rem(y + 3, 4), lax.rem(y + 2, 4)
-    dev_up, dev_down = (dp, x, up), (dp, x, down)
+    dev_up, dev_down, dev_far = (dp, x, up), (dp, x, down), (dp, x, far)
+    iz, ic = lax.div(dp, 2), lax.rem(dp, 2)
+    n_z = z.n_z
+    z_up, z_down = lax.rem(iz + 1, n_z), lax.rem(iz + n_z - 1, n_z)
+    dev_zup, dev_zdown = (2 * z_up + ic, x, y), (2 * z_down + ic, x, y)
+    dev_twin = (2 * iz + 1 - ic, x, y)
 
     def wcopy(i):
         if i == 0:
@@ -112,6 +131,7 @@
     lax.fori_loop(1, n_x, greet_x, 0)
     pl.semaphore_signal(barrier, inc=1, device_id=dev_up, device_id_type=MESH)
     pl.semaphore_signal(barrier, inc=1, device_id=dev_down, device_id_type=MESH)
+    pl.semaphore_signal(barrier, inc=1, device_id=dev_far, device_id_type=MESH)
 
     slot = lax.broadcasted_iota(jnp.int32, (rows, z.tok), 0)
     s_x = slot >> log2(xb)
@@ -141,7 +161,13 @@
 
     choose(1)
 
-    pl.semaphore_wait(barrier, n_dp - 1 + n_x - 1 + 2)
+    for b in range(z.late):
+        tb[b, y, iz, ic] = dy_ref[:, (mix - z.late + b) * CW : (mix - z.late + b + 1) * CW]
+    l_row = lax.broadcasted_iota(jnp.int32, (z.tok, LANES), 0)
+    l_col = lax.broadcasted_iota(jnp.int32, (z.tok, LANES), 1)
+    pmy[y] = dot_nn(place_ref[...], onehot(l_col == l_row + y * z.tok)).astype(BF16)
+
+    pl.semaphore_wait(barrier, n_dp - 1 + n_x - 1 + 3)
 
     def remote(src, dst, send, recv, dev):
         return pltpu.make_async_remote_copy(
@@ -213,7 +239,9 @@
             for o in range(4):
                 gt[o] = g[q, o, :, cs].astype(F32)
             return
-
+        multiply(q)
+
+    def multiply(q):
         @pl.when(q == 1)
         def _():
             def one(o, c):
@@ -268,7 +296,7 @@
 
             lax.fori_loop(0, 4, one, 0)
 
-        pl.when(jnp.logical_and(q > mix, q < z.fwd - 1))(functools.partial(grad_down, q))
+        pl.when(jnp.logical_and(q > mix, q != z.early - 1))(functools.partial(grad_down, q))
 
     def grad_down(q):
         j = q - mix - 1
@@ -286,10 +314,125 @@
 
     def at(t, do):
         pl.when(t == 0)(functools.partial(do, t, LANES))
-        pl.when(jnp.logical_and(t > 0, t < z.fwd))(functools.partial(do, t, CW))
+        pl.when(jnp.logical_and(t > 0, t < z.early))(functools.partial(do, t, CW))
+
+    def spread():
+        for b in range(z.late):
+            own = tb.at[b, y, iz, ic]
+            for dev in (dev_up, dev_down, dev_far):
+                remote(own, own, by_s.at[b], by_r.at[b], dev).start()
+        for dev in (dev_up, dev_down, dev_far):
+            remote(pmy.at[y], pmy.at[y], pm_s.at[0], pm_r.at[0], dev).start()
+
+    def share_places():
+        got(pmy.at[pl.ds(0, 3)], pm_r.at[0])
+        places = pmy[0] + pmy[1] + pmy[2] + pmy[3]
+        pmd[...] = dot_nn(mats[0], places).astype(BF16)
+        mine = pl.ds(pl.multiple_of(dp * db, 16), db)
+
+        def send(j, c):
+            to = lax.rem(dp + j, n_dp)
+            remote(
+                pmd.at[pl.ds(pl.multiple_of(to * db, 16), db)], mb.at[mine],
+                mb_s.at[0], mb_r.at[0], (to, x, y),
+            ).start()
+            return c
+
+        lax.fori_loop(1, n_dp, send, 0)
+        mb[mine] = pmd[mine]
+
+    def make_picks():
+        got(mb.at[pl.ds(0, rows - db)], mb_r.at[0])
+        k_row = lax.broadcasted_iota(jnp.int32, (LANES, LANES), 0)
+        k_col = lax.broadcasted_iota(jnp.int32, (LANES, LANES), 1)
+        same = (k_row >> log2(z.tok)) == (k_col >> log2(z.tok))
+        count = jnp.where(same, ((k_row & (z.tok - 1)) + 1).astype(F32), 0.0)
+        numbers = dot_nn(mb[...], count.astype(BF16)).astype(BF16)
+        numbers = dot_nn(mats[1], numbers)
+        p_row = lax.broadcasted_iota(jnp.int32, (rows, n_dp * z.tok), 0)
+        p_col = lax.broadcasted_iota(jnp.int32, (rows, n_dp * z.tok), 1)
+        first = ((p_row & (xb - 1)) >> log2(cap)) * z.tok
+        number = (p_col - first + 1).astype(F32)
+        for o in range(4):
+            found = numbers[:, o * z.tok : o * z.tok + 1]
+            pick[o] = onehot(jnp.logical_and(number == found, found > 0.0))
+
+    n_ring = n_z // 2
+
+    def ring_send(b, s):
+        block_up = lax.rem(iz + n_z - (s - 1), n_z)
+        block_down = lax.rem(iz + (s - 1), n_z)
+        some_up, some_down = (0, 4), (0, 4)
+        if s == n_ring:
+            some_up, some_down = (0, 2), (2, 2)
+        a = tb.at[b, pl.ds(*some_up), block_up, ic]
+        remote(a, a, bz_s.at[b], bu_r.at[b, s - 1], dev_zup).start()
+        a = tb.at[b, pl.ds(*some_down), block_down, ic]
+        remote(a, a, bz_s.at[b], bd_r.at[b, s - 1], dev_zdown).start()
+
+    def ring_got(b, s):
+        block_up = lax.rem(iz + n_z - s, n_z)
+        block_down = lax.rem(iz + s, n_z)
+        some_up, some_down = (0, 4), (0, 4)
+        if s == n_ring:
+            some_up, some_down = (0, 2), (2, 2)
+        got(tb.at[b, pl.ds(*some_up), block_up, ic], bu_r.at[b, s - 1])
+        got(tb.at[b, pl.ds(*some_down), block_down, ic], bd_r.at[b, s - 1])
+
+    def b_ring(s, b):
+        if s == 0:
+            got(tb.at[b, pl.ds(0, 3), iz, ic], by_r.at[b])
+        else:
+            ring_got(b, s)
+        if s < n_ring:
+            ring_send(b, s + 1)
+        else:
+            a = tb.at[b, :, :, ic]
+            remote(a, a, bs_s.at[b], bs_r.at[b], dev_twin).start()
+
+    def b_select(b):
+        got(tb.at[b, :, :, 1 - ic], bs_r.at[b])
+        mine = pl.ds(pl.multiple_of(x * xb, 16), xb)
+
+        def one(o, c):
+            bsel[b, o] = dot_nn(pick[o], tb[b, o].reshape(n_dp * z.tok, CW)).astype(BF16)
+            bx[b, o, mine] = bsel[b, o, mine]
+
+            def send(j, c):
+                to = lax.rem(x + j, n_x)
+                remote(
+                    bsel.at[b, o, pl.ds(pl.multiple_of(to * xb, 16), xb)], bx.at[b, o, mine],
+                    bx_s.at[b], bx_r.at[b], (dp, to, y),
+                ).start()
+                return c
+
+            return lax.fori_loop(1, n_x, send, c)
+
+        lax.fori_loop(0, 4, one, 0)
+
+    def b_place(b):
+        got(bx.at[b, :, pl.ds(0, rows - xb)], bx_r.at[b])
+
+        def one(o, c):
+            g[z.early + b, o] = dot_nn(mats[0], bx[b, o]).astype(BF16)
+            return c
+
+        lax.fori_loop(0, 4, one, 0)
+
+    def b_multiply(b):
+        multiply(z.early + b)
+
+    def when_b(t, start, stride, do):
+        u = t - start
+        on = jnp.logical_and(u >= 0, u < stride * z.late)
+        if stride > 1:
+            on = jnp.logical_and(on, lax.rem(u + stride * z.late, stride) == 0)
+        pl.when(on)(lambda: do(lax.div(u, stride)))
 
     f0(0, LANES)
-    for q in range(1, AHEAD):
+    f0(jnp.int32(1), CW)
+    spread()
+    for q in range(2, min(AHEAD, z.early)):
         f0(jnp.int32(q), CW)
     pt[...] = dot_nt(onehot(t_row == t_col), place_ref[...]).astype(BF16)
     i_row = lax.broadcasted_iota(jnp.int32, (rows, rows), 0)
@@ -307,15 +450,26 @@
     for i in range(2 + mix):
         wcopy(i).wait()
 
+    t_sel = B_START + B_STEP * n_ring + 1
+    t_place = t_sel + B_X
+    t_mul = max(t_place + (B_STEP - 1) * (z.late - 1) + 1, mix + LAGS[2] + 2)
+
     def tick_out(t, c):
-        at(t - 4, f3)
-        at(t - 2, f2)
+        at(t - LAGS[1], f3)
+        at(t - LAGS[0], f2)
         at(t, f1)
-        pl.when(t + AHEAD < z.fwd)(functools.partial(f0, t + AHEAD, CW))
-        at(t - 5, f4)
+        pl.when(t + AHEAD < z.early)(functools.partial(f0, t + AHEAD, CW))
+        at(t - LAGS[2], f4)
+        for s in range(n_ring + 1):
+            when_b(t, B_START + B_STEP * s, B_STEP, functools.partial(b_ring, s))
+        pl.when(t == B_START)(share_places)
+        pl.when(t == t_sel - 1)(make_picks)
+        when_b(t, t_sel, B_STEP, b_select)
+        when_b(t, t_place, B_STEP, b_place)
+        when_b(t, t_mul, 1, b_multiply)
         return c
 
-    lax.fori_loop(0, z.fwd + 5, tick_out, 0)
+    lax.fori_loop(0, max(z.early + LAGS[2], t_mul + z.late), tick_out, 0)
 
     def middle(o):
         back_h = bh[o]
@@ -428,7 +582,7 @@
     r0(0, CW)
     for o in (down, up, y):
         middle(o)
-    grad_down(z.fwd - 1)
+    grad_down(z.early - 1)
     lax.fori_loop(1, z.ret + 8, tick_back, 0)
 
     def drain_out(q, w):
@@ -445,8 +599,15 @@
         left(sx.at[r, pl.ds(0, rows - xb), cs], sx_s.at[r])
 
     drain_out(0, LANES)
-    for q in range(1, z.fwd):
+    for q in range(1, z.early):
         drain_out(q, CW)
+    for b in range(z.late):
+        left(tb.at[b, pl.ds(0, 3), 0, 0], by_s.at[b])
+        left(tb.at[b, :, pl.ds(0, n_z - 1), 0], bz_s.at[b])
+        left(tb.at[b, :, :, 0], bs_s.at[b])
+        left(bx.at[b, :, pl.ds(0, rows - xb)], bx_s.at[b])
+    left(pmy.at[pl.ds(0, 3)], pm_s.at[0])
+    left(mb.at[pl.ds(0, rows - db)], mb_s.at[0])
     for j in range(mix):
         down_copy(j).wait()
     for r in range(mix):
@@ -477,6 +638,7 @@
 
 def body(cap, tokens, out_grad, routes, gates, w_gate, w_up, w_down):
     z = Sizes(
+        late=min(LATE, tokens.shape[1] // CW - 1),
         n_dp=lax.axis_size("dp"), n_x=lax.axis_size("expert"), tok=tokens.shape[0],
         top=routes.shape[1], cap=cap, width=tokens.shape[1], ff=w_gate.shape[2],
     )
@@ -517,6 +679,17 @@
         vm((ret, rows, CW), BF16),
         vm((ret, rows, CW), BF16),
         vm((ret, rows, CW), BF16),
+        vm((z.late, 4, z.n_z, 2, z.tok, CW), BF16),
+        vm((4, rows, LANES), BF16),
+        vm((rows, LANES), BF16),
+        vm((rows, LANES), BF16),
+        vm((4, rows, z.n_dp * z.tok), BF16),
+        vm((z.late, 4, rows, CW), BF16),
+        vm((z.late, 4, rows, CW), BF16),
+        sem((z.late,)), sem((z.late,)),
+        sem((z.late, z.n_z // 2)), sem((z.late, z.n_z // 2)), sem((z.late,)),
+        sem((z.late,)), sem((z.late,)), sem((z.late,)), sem((z.late,)),
+        sem((1,)), sem((1,)), sem((1,)), sem((1,)),
         sem((2 + mix,)),
         sem((mix,)),
     ] + [sem((fwd,))] * 9 + [sem((ret,))] * 10

time: 154 us -> 146 us (0.948)
  Pallas kernels: 153 us -> 145 us
    pallas_call x1, Pallas kernels: 150 us -> 142 us  [body(): pl.pallas_call(functools.partial(kernel, z), out_shape=(jax.ShapeDtypeStr...]
where the time goes in v4:
time: 146 us
  Pallas kernels  145 us (99%)
    pallas_call x1, Pallas kernels, body(): pl.pallas_call(functools.partial(kernel, z), out_shape=(jax.ShapeDtypeStr...  142 us

profile of v4, /device:TPU:1, one launch (start us, length us, event | category | flops | bytes accessed | tf_op | source)
XLA Modules:
  0.0 145.6 jit_solution(4010288402170669643)
XLA Ops:
  0.6 142.1 %shard_map.94 = (bf16[32,2048]{1,0:T(8,128)(2,1)}, bf16[6,32]{1,0:T(8,128)(2,1)}, f32[352,2048]{1,0:T(8,128)}) custom-call(s32[6,32]{1,0:T(8,128)} %bitcast.14, bf16[6,32]{1,0:T(8,128)(2,1)} %bitcast.15, bf16[32,2048]{1,0:T(8,128)(2,1)} %tok_ref.1, bf16[32,2048]{1,0:T(8,128)(2,1)} %dy_ref.1, bf16[352,2048]{1,0:T(8,128)(2,1)} %bitcast.11, ...), custom_call_target="tpu_custom_call" | custom-call | tf_op jit(solution)/shard_map/pallas_call | solution.py:698
  142.7 2.9 %shard_map.95 = (bf16[32,2048]{1,0:T(8,128)(2,1)}, bf16[6,32]{1,0:T(8,128)(2,1)}, f32[352,2048]{1,0:T(8,128)}) custom-call(bf16[32,2048]{1,0:T(8,128)(2,1)} %get-tuple-element.9.tok_in, bf16[6,32]{1,0:T(8,128)(2,1)} %get-tuple-element.10.gate_in, f32[352,2048]{1,0:T(8,128)} %get-tuple-element.11.down_in), custom_call_target="tpu_custom_call" | custom-call | tf_op jit(solution)/shard_map/pallas_call | solution.py:713

commit v5 on v4

--- a/solution.py
+++ b/solution.py
@@ -16,7 +16,7 @@
 LATE = 2
 AHEAD = 4
 LAGS = (3, 5, 6)
-B_START, B_STEP, B_X = 3, 2, 3
+B_START, B_STEP, B_X, B_GAP = 3, 2, 3, 1
 
 
 @dataclasses.dataclass(frozen=True)
@@ -73,9 +73,9 @@
 
 
 def kernel(
-    z, routes_ref, gates_ref, tok_ref, dy_ref, wg_hbm, wu_hbm, wd_hbm,
+    z, routes_hbm, gates_ref, tok_hbm, dy_hbm, wg_hbm, wu_hbm, wd_hbm,
     out_tok, out_gate, down_hbm,
-    out_down, place_ref, xc, sel, rx, sd, g, wg, wu, wd, pg, pu, hf, ht, bh, gt, gg, gu, gp, mats, pt,
+    routes_ref, tok_ref, dy_ref, in_sem, out_down, place_ref, xc, sel, rx, sd, g, wg, wu, wd, pg, pu, hf, ht, bh, gt, gg, gu, gp, mats, pt,
     os_, ora, orb, am, ap, arp, arm, rd, rb, sx, hb,
     tb, pmy, pmd, mb, pick, bsel, bx,
     by_s, by_r, bu_r, bd_r, bz_s, bs_s, bs_r, bx_s, bx_r, pm_s, pm_r, mb_s, mb_r,
@@ -110,8 +110,14 @@
         cols = pl.ds(pl.multiple_of(j * CW, CW), CW)
         return pltpu.make_async_copy(out_down.at[:, cols], down_hbm.at[:, cols], d_sem.at[j])
 
-    for i in range(2 + mix):
-        wcopy(i).start()
+    reads = [
+        pltpu.make_async_copy(a, b, in_sem.at[i])
+        for i, (a, b) in enumerate(
+            [(routes_hbm, routes_ref), (tok_hbm, tok_ref), (dy_hbm, dy_ref)]
+        )
+    ]
+    for read in reads:
+        read.start()
 
     barrier = pltpu.get_barrier_semaphore()
 
@@ -133,17 +139,23 @@
     pl.semaphore_signal(barrier, inc=1, device_id=dev_down, device_id_type=MESH)
     pl.semaphore_signal(barrier, inc=1, device_id=dev_far, device_id_type=MESH)
 
+    for i in range(2 + mix):
+        wcopy(i).start()
+    for read in reads:
+        read.wait()
+
     slot = lax.broadcasted_iota(jnp.int32, (rows, z.tok), 0)
     s_x = slot >> log2(xb)
     s_dp = (slot & (xb - 1)) >> log2(cap)
     s_rank = slot & (cap - 1)
     s_e = s_dp * n_x + s_x
+    gates = gates_ref[...].astype(F32)
     named = jnp.zeros((rows, z.tok), F32)
     gate = jnp.zeros((rows, z.tok), F32)
     for k in range(z.top):
         hit = routes_ref[k : k + 1, :] == s_e
         named = jnp.where(hit, 1.0, named)
-        gate = jnp.where(hit, gates_ref[k : k + 1, :].astype(F32), gate)
+        gate = jnp.where(hit, gates[k : k + 1, :], gate)
     t_row = lax.broadcasted_iota(jnp.int32, (z.tok, z.tok), 0)
     t_col = lax.broadcasted_iota(jnp.int32, (z.tok, z.tok), 1)
     rank = dot_nn(named.astype(BF16), onehot(t_row < t_col))
@@ -452,7 +464,7 @@
 
     t_sel = B_START + B_STEP * n_ring + 1
     t_place = t_sel + B_X
-    t_mul = max(t_place + (B_STEP - 1) * (z.late - 1) + 1, mix + LAGS[2] + 2)
+    t_mul = max(t_place + (B_GAP - 1) * (z.late - 1) + 1, mix + LAGS[2] + 2)
 
     def tick_out(t, c):
         at(t - LAGS[1], f3)
@@ -461,11 +473,11 @@
         pl.when(t + AHEAD < z.early)(functools.partial(f0, t + AHEAD, CW))
         at(t - LAGS[2], f4)
         for s in range(n_ring + 1):
-            when_b(t, B_START + B_STEP * s, B_STEP, functools.partial(b_ring, s))
+            when_b(t, B_START + B_STEP * s, B_GAP, functools.partial(b_ring, s))
         pl.when(t == B_START)(share_places)
         pl.when(t == t_sel - 1)(make_picks)
-        when_b(t, t_sel, B_STEP, b_select)
-        when_b(t, t_place, B_STEP, b_place)
+        when_b(t, t_sel, B_GAP, b_select)
+        when_b(t, t_place, B_GAP, b_place)
         when_b(t, t_mul, 1, b_multiply)
         return c
 
@@ -560,36 +572,59 @@
         e_col = lax.broadcasted_iota(jnp.int32, (LANES, LANES), 1)
         by_expert = dot_nt(onehot(e_row == e_col), by_expert.astype(BF16))
         e_tok = lax.broadcasted_iota(jnp.int32, (LANES, z.tok), 0)
-        for k in range(z.top):
-            hit = routes_ref[k : k + 1, :] == e_tok
-            out_gate[k : k + 1, :] = jnp.sum(
-                jnp.where(hit, by_expert, 0.0), axis=0, keepdims=True
-            ).astype(BF16)
+        out_gate[...] = jnp.concatenate(
+            [
+                jnp.sum(
+                    jnp.where(routes_ref[k : k + 1, :] == e_tok, by_expert, 0.0),
+                    axis=0, keepdims=True,
+                )
+                for k in range(z.top)
+            ],
+            axis=0,
+        ).astype(BF16)
 
     def back(t, do):
         pl.when(jnp.logical_and(t >= 0, t < mix))(functools.partial(do, t, CW))
         pl.when(t == mix)(functools.partial(do, t, LANES))
 
+    def drain_out(q, w):
+        cs = pl.ds(0, w)
+        left(sel.at[q, pl.ds(0, rows - xb), cs], xs.at[q])
+        left(sd.at[q, pl.ds(0, rows - db), cs], ds_.at[q])
+        left(g.at[q, pl.ds(0, 3), :, cs], ys.at[q])
+
+    def drain_all_out():
+        drain_out(0, LANES)
+        for q in range(1, z.early):
+            drain_out(q, CW)
+        for b in range(z.late):
+            left(tb.at[b, pl.ds(0, 3), 0, 0], by_s.at[b])
+            left(tb.at[b, :, pl.ds(0, n_z - 1), 0], bz_s.at[b])
+            left(tb.at[b, :, :, 0], bs_s.at[b])
+            left(bx.at[b, :, pl.ds(0, rows - xb)], bx_s.at[b])
+        left(pmy.at[pl.ds(0, 3)], pm_s.at[0])
+        left(mb.at[pl.ds(0, rows - db)], mb_s.at[0])
+
+    def rest():
+        middle(y)
+        grad_down(z.early - 1)
+
     def tick_back(t, c):
         back(t - 2, r1)
         back(t, r0)
+        pl.when(t == 3)(rest)
         back(t - 4, r2)
         back(t - 6, r3)
         back(t - 8, r4)
+        pl.when(t == 5)(drain_all_out)
         return c
 
     middle(far)
     r0(0, CW)
-    for o in (down, up, y):
-        middle(o)
-    grad_down(z.early - 1)
-    lax.fori_loop(1, z.ret + 8, tick_back, 0)
-
-    def drain_out(q, w):
-        cs = pl.ds(0, w)
-        left(sel.at[q, pl.ds(0, rows - xb), cs], xs.at[q])
-        left(sd.at[q, pl.ds(0, rows - db), cs], ds_.at[q])
-        left(g.at[q, pl.ds(0, 3), :, cs], ys.at[q])
+    r0(1, CW)
+    middle(down)
+    middle(up)
+    lax.fori_loop(2, z.ret + 8, tick_back, 0)
 
     def drain_back(r, w):
         cs = pl.ds(0, w)
@@ -598,16 +633,6 @@
         left(rd.at[r, pl.ds(0, rows - db), cs], rd_s.at[r])
         left(sx.at[r, pl.ds(0, rows - xb), cs], sx_s.at[r])
 
-    drain_out(0, LANES)
-    for q in range(1, z.early):
-        drain_out(q, CW)
-    for b in range(z.late):
-        left(tb.at[b, pl.ds(0, 3), 0, 0], by_s.at[b])
-        left(tb.at[b, :, pl.ds(0, n_z - 1), 0], bz_s.at[b])
-        left(tb.at[b, :, :, 0], bs_s.at[b])
-        left(bx.at[b, :, pl.ds(0, rows - xb)], bx_s.at[b])
-    left(pmy.at[pl.ds(0, 3)], pm_s.at[0])
-    left(mb.at[pl.ds(0, rows - db)], mb_s.at[0])
     for j in range(mix):
         down_copy(j).wait()
     for r in range(mix):
@@ -615,8 +640,8 @@
     drain_back(mix, LANES)
 
 
-def hand_over(tok_in, gate_in, down_in, tok_out, gate_out, down_out, tok, gate, down, sem):
-    parts = [(tok_in, tok, tok_out), (gate_in, gate, gate_out)]
+def hand_over(tok_in, gate_in, down_in, tok_out, gate_out, down_out, tok, down, sem):
+    parts = [(tok_in, tok, tok_out)]
     step = down.shape[0] // 4
     for i in range(4):
         part = pl.ds(i * step, step)
@@ -629,6 +654,7 @@
     ]
     for read in reads:
         read.start()
+    gate_out[...] = gate_in[...]
     for read, write in zip(reads, writes):
         read.wait()
         write.start()
@@ -647,6 +673,10 @@
     vm = pltpu.VMEM
     sem = pltpu.SemaphoreType.DMA
     scratch = [
+        vm(routes.T.shape, routes.dtype),
+        vm(tokens.shape, tokens.dtype),
+        vm(out_grad.shape, out_grad.dtype),
+        sem((3,)),
         vm((z.ff, z.width), F32),
         vm((rows, z.tok), BF16),
         vm((fwd, z.tok, CW), BF16),
@@ -702,7 +732,7 @@
             jax.ShapeDtypeStruct((z.top, z.tok), BF16),
             jax.ShapeDtypeStruct((z.ff, z.width), F32),
         ),
-        in_specs=[vmem] * 4 + [hbm] * 3,
+        in_specs=[hbm, vmem] + [hbm] * 5,
         out_specs=(vmem, vmem, hbm),
         scratch_shapes=scratch,
         compiler_params=pltpu.CompilerParams(
@@ -713,9 +743,11 @@
     grad_tokens, grad_gate, grad_down = pl.pallas_call(
         hand_over,
         out_shape=tuple(jax.ShapeDtypeStruct(r.shape, r.dtype) for r in results),
-        in_specs=[hbm] * 3,
-        out_specs=(hbm,) * 3,
-        scratch_shapes=[vm(r.shape, r.dtype) for r in results] + [sem((2, 6))],
+        in_specs=[hbm, vmem, hbm],
+        out_specs=(hbm, vmem, hbm),
+        scratch_shapes=[
+            vm(grad_tokens.shape, BF16), vm(grad_down.shape, F32), sem((2, 5)),
+        ],
     )(*results)
     return grad_tokens, grad_gate.T, grad_down[None]
 

time: 146 us -> 147 us (level)
  no operation moved by 1% of the time
where the time goes in v5:
time: 147 us
  Pallas kernels  146 us (99%)
    pallas_call x1, Pallas kernels, body(): pl.pallas_call(functools.partial(kernel, z), out_shape=(jax.ShapeDtypeStr...  142 us
    pallas_call x1, Pallas kernels, body(): pl.pallas_call(hand_over, out_shape=tuple((jax.ShapeDtypeStruct(r.shape,...  4.08 us

profile of v5, /device:TPU:1, one launch (start us, length us, event | category | flops | bytes accessed | tf_op | source)
XLA Modules:
  0.0 146.8 jit_solution(11034018301589317884)
XLA Ops:
  0.6 142.1 %shard_map.94 = (bf16[32,2048]{1,0:T(8,128)(2,1)}, bf16[6,32]{1,0:T(8,128)(2,1)}, f32[352,2048]{1,0:T(8,128)}) custom-call(s32[6,32]{1,0:T(8,128)} %bitcast.14, bf16[6,32]{1,0:T(8,128)(2,1)} %bitcast.15, bf16[32,2048]{1,0:T(8,128)(2,1)} %tok_hbm.1, bf16[32,2048]{1,0:T(8,128)(2,1)} %dy_hbm.1, bf16[352,2048]{1,0:T(8,128)(2,1)} %bitcast.11, ...), custom_call_target="tpu_custom_call" | custom-call | tf_op jit(solution)/shard_map/pallas_call | solution.py:728
  142.7 4.1 %shard_map.95 = (bf16[32,2048]{1,0:T(8,128)(2,1)}, bf16[6,32]{1,0:T(8,128)(2,1)}, f32[352,2048]{1,0:T(8,128)}) custom-call(bf16[32,2048]{1,0:T(8,128)(2,1)} %get-tuple-element.9.tok_in, bf16[6,32]{1,0:T(8,128)(2,1)} %get-tuple-element.10.gate_in, f32[352,2048]{1,0:T(8,128)} %get-tuple-element.11.down_in), custom_call_target="tpu_custom_call" | custom-call | tf_op jit(solution)/shard_map/pallas_call | solution.py:743
